TPU v7x, 256 devices: a whole 4x4x8 slice. The times are simulated.
256 devices in a mesh: tile: 16 (over y_lo, z), tf: 16 (over x, y_hi, core).
Axes of the slice: x: 4, y: 4 (y_hi: 2, y_lo: 2; y = y_hi * 2 + y_lo), z: 8, core: 2. Of those that a mesh axis runs over, the one named last changes fastest.
Arguments:
- test_field: float32 [16, 3, 16, 256, 1024], P('tf', None, None, 'tile'), may hold values from -6 to 6
- register: float32 [16, 3, 16, 256, 1024], P('tf', None, None, 'tile'), may hold values from -6 to 6
- velocity: bfloat16 [3, 16, 256, 1024], P(None, 'tf', 'tile'), may hold values from -6 to 6
- shear_shift: int32 [2], replicated, may hold values from 0 to 255
Outputs:
- new_field: float32 [16, 3, 16, 256, 1024], P('tf', None, None, 'tile')
- new_register: float32 [16, 3, 16, 256, 1024], P('tf', None, None, 'tile')
Inputs may be any that keep to these rules, and one draw needn't show every extreme that they name: `shear_shift`: the two offsets are independent.
All inputs are finite; a program needn't handle non-finite values.
Results may differ from a plain program's by a relative error of at most 0.0065.
Values may be sent and summed in bfloat16 or wider, within the bound.
A program may use at most 128 MiB of HBM per device.

v0:
```python
import math

import jax
import jax.numpy as jnp
from jax import lax
from jax.sharding import PartitionSpec as P

DIFFUSIVITY = 0.1
TIME_STEP = 0.3
RK_ALPHA = -5.0 / 9.0
RK_BETA = 15.0 / 16.0
SWEEP_SPEED = 0.75
STRETCH_RATE = 0.375


def with_halo(x, sides, width):
    for axis, dim in sides:
        size, length = (lax.axis_size(axis), x.shape[dim])
        up = [(i, (i + 1) % size) for i in range(size)]
        down = [(j, i) for i, j in up]
        last = lax.slice_in_dim(x, length - width, length, axis=dim)
        initial = lax.slice_in_dim(x, 0, width, axis=dim)
        before = lax.ppermute(last, axis, up)
        after = lax.ppermute(initial, axis, down)
        x = jnp.concatenate([before, x, after], axis=dim)
    return x


def first_derivative(shifted):
    return (
        45.0 * (shifted(1) - shifted(-1))
        - 9.0 * (shifted(2) - shifted(-2))
        + (shifted(3) - shifted(-3))
    ) / 60.0


def second_derivative(shifted):
    return (
        -49.0 / 18.0 * shifted(0)
        + 1.5 * (shifted(1) + shifted(-1))
        - 0.15 * (shifted(2) + shifted(-2))
        + (shifted(3) + shifted(-3)) / 90.0
    )


def test_pattern(field_index, planes):
    height = jnp.arange(planes).astype(jnp.float32)
    wavenumber = (field_index // 4 + 1).astype(jnp.float32)
    phase = 2.0 * math.pi * wavenumber[:, None] * height[None, :] / planes
    profile = jnp.where((field_index // 2 % 2 == 0)[:, None], jnp.cos(phase), jnp.sin(phase))
    component = field_index % 2
    selector = (jnp.arange(3)[None, :] == component[:, None]).astype(jnp.float32)
    return (selector[:, :, None] * profile[:, None, :])[:, :, :, None, None]


def cross_emf(velocity, summed):
    vel = velocity.astype(jnp.float32)
    fld = summed.astype(jnp.float32)
    emf_x = vel[1] * fld[:, 2] - vel[2] * fld[:, 1]
    emf_y = vel[2] * fld[:, 0] - vel[0] * fld[:, 2]
    emf_z = vel[0] * fld[:, 1] - vel[1] * fld[:, 0]
    return jnp.stack([emf_x, emf_y, emf_z], 1).astype(jnp.bfloat16)


def tendency(field, view, width):

    def deriv(name, axis, channel):

        def shifted(offset):
            return view(name, axis, offset, channel)

        return first_derivative(shifted)

    def second(axis):

        def shifted(offset):
            return view("field", axis, offset, slice(None))

        return second_derivative(shifted)

    curl_x = deriv("emf", 1, 2) - deriv("emf", 2, 1)
    curl_y = deriv("emf", 2, 0) - deriv("emf", 0, 2)
    curl_z = deriv("emf", 0, 1) - deriv("emf", 1, 0)
    curl = jnp.stack([curl_x, curl_y, curl_z], 1)
    laplace = second(0) + second(1) + second(2)
    field_dy = deriv("field", 1, slice(None))
    xpos = jnp.arange(width).astype(jnp.float32)
    sweep = -SWEEP_SPEED * (2.0 * xpos / (width - 1) - 1.0)
    rate = curl + DIFFUSIVITY * laplace - sweep * field_dy
    return rate.at[:, 1].add(-STRETCH_RATE * field[:, 0])


def make_emf(summed, velocity):
    whole_velocity = lax.all_gather(velocity, "tf", axis=1, tiled=True)
    return cross_emf(whole_velocity, summed)


def body(test_field, register, velocity, shear_shift):
    fields_here = test_field.shape[0]
    rows_here = test_field.shape[3]
    width = test_field.shape[4]
    planes = test_field.shape[2]
    field_index = lax.axis_index("tf") * fields_here + jnp.arange(fields_here)
    pattern = test_pattern(field_index, planes)
    field_rows = with_halo(test_field.astype(jnp.bfloat16), (("tile", 3),), 3).astype(
        test_field.dtype
    )
    summed = (test_field + pattern).astype(jnp.bfloat16)
    emf = make_emf(summed, velocity)
    emf_rows = with_halo(emf, (("tile", 3),), 3)
    lower_source = jnp.concatenate(
        [test_field[..., width - 3 :], emf[..., width - 3 :].astype(jnp.float32)], axis=1
    )
    upper_source = jnp.concatenate([test_field[..., :3], emf[..., :3].astype(jnp.float32)], axis=1)
    strips = jnp.stack([lower_source, upper_source], 1)
    tiles = lax.axis_size("tile")
    whole_strips = lax.all_gather(strips.astype(jnp.bfloat16), "tile", axis=4, tiled=True).astype(
        strips.dtype
    )
    doubled = jnp.concatenate([whole_strips, whole_strips], axis=4)
    total_rows = rows_here * tiles
    sides = []
    for side in range(2):
        start = (lax.axis_index("tile") * rows_here + shear_shift[side]) % total_rows
        sides.append(lax.dynamic_slice_in_dim(doubled[:, side], start, rows_here, 3))
    lower_ghost = sides[0]
    upper_ghost = sides[1]
    padded = {
        "field": jnp.concatenate([lower_ghost[:, :3], test_field, upper_ghost[:, :3]], axis=-1),
        "emf": jnp.concatenate(
            [lower_ghost[:, 3:].astype(jnp.bfloat16), emf, upper_ghost[:, 3:].astype(jnp.bfloat16)],
            axis=-1,
        ),
    }
    rowed = {"field": field_rows, "emf": emf_rows}
    arrays = {"field": test_field, "emf": emf}

    def view(name, axis, offset, channel):
        if axis == 0:
            return padded[name][:, channel][..., 3 + offset : 3 + offset + width].astype(
                jnp.float32
            )
        if axis == 1:
            return lax.slice_in_dim(
                rowed[name][:, channel],
                3 + offset,
                3 + offset + rows_here,
                axis=rowed[name][:, channel].ndim - 2,
            ).astype(jnp.float32)
        return jnp.roll(arrays[name][:, channel], -offset, axis=-3).astype(jnp.float32)

    rate = tendency(test_field, view, width)
    new_register = RK_ALPHA * register + TIME_STEP * rate
    new_field = test_field + RK_BETA * new_register
    return (new_field, new_register)


def solution(mesh):
    return jax.shard_map(
        body,
        mesh=mesh,
        in_specs=(
            P("tf", None, None, "tile", None),
            P("tf", None, None, "tile", None),
            P(None, "tf", "tile", None),
            P(),
        ),
        out_specs=(P("tf", None, None, "tile", None), P("tf", None, None, "tile", None)),
        check_vma=False,
    )
```

profile of v0, /device:TPU:32, one launch (start us, length us, event | category | flops | bytes accessed | tf_op | source)
XLA Modules:
  0.0 211.0 jit_solution(14419312792183972771)
XLA Ops:
  7.2 0.7 all-gather.2.cloned.1.call-update
  7.9 3.8 %copy.196 = bf16[1,3,16,16,1024]{4,2,3,1,0:T(8,128)(2,1)S(1)} copy(f32[1,3,16,16,1024]{4,3,2,1,0:T(8,128)} %param.6) | data formatting | bytes 4718592 | tf_op args[0]
  11.7 1.2 copy-done.8
  12.9 0.9 fusion.42
  13.7 1.9 collective-permute-start.2
  15.7 0.8 fusion.39
  16.5 1.1 fusion.43
  17.8 0.7 fusion.58
  18.5 1.0 fusion.37
  19.5 1.9 fusion.27
  21.4 3.1 %fusion.36 = (f32[1,3,13,16,1024]{4,3,2,1,0:T(8,128)}, f32[1,3,13,16,1024]{4,3,2,1,0:T(8,128)}) fusion(f32[1,3,16,16,1024]{4,3,2,1,0:T(8,128)S(1)} %copy-done), kind=kLoop, calls=%fused_computation.87 | loop fusion | bytes 10223616 | tf_op jit(solution)/shard_map/jit(_roll_static)/slice | solution.py:150
  24.5 3.4 %fusion.38 = (f32[1,3,14,16,1024]{4,3,2,1,0:T(8,128)}, f32[1,3,14,16,1024]{4,3,2,1,0:T(8,128)}) fusion(f32[1,3,16,16,1024]{4,3,2,1,0:T(8,128)S(1)} %copy-done), kind=kLoop, calls=%fused_computation.89 | loop fusion | bytes 11010048 | tf_op jit(solution)/shard_map/jit(_roll_static)/slice | solution.py:150
  27.8 3.5 %fusion.40 = (f32[1,3,15,16,1024]{4,3,2,1,0:T(8,128)}, f32[1,3,15,16,1024]{4,3,2,1,0:T(8,128)}) fusion(f32[1,3,16,16,1024]{4,3,2,1,0:T(8,128)S(1)} %copy-done), kind=kLoop, calls=%fused_computation.91 | loop fusion | bytes 11796480 | tf_op jit(solution)/shard_map/jit(_roll_static)/slice | solution.py:150
  32.7 1.0 copy.179
  33.7 1.0 copy.181
  34.7 1.1 fusion.35
  35.9 0.7 copy-done.9
  36.5 1.3 pad_maximum_fusion.2
  37.9 3.5 %copy_convert_fusion.1 = f32[1,3,16,22,1024]{4,3,2,1,0:T(8,128)} fusion(bf16[1,3,16,22,1024]{4,2,3,1,0:T(8,128)(2,1)S(1)} %pad_maximum_fusion.2), kind=kLoop, calls=%fused_computation.45 | loop fusion | flops 1081344 | bytes 6488064 | tf_op jit(solution)/shard_map/convert_element_type | solution.py:105
  41.3 23.8 %all-gather.2.cloned.1.call-done = bf16[3,16,16,1024]{3,2,0,1:T(8,128)(2,1)} async-done(((bf16[3,1,16,1024]{3,2,0,1:T(8,128)(2,1)}), bf16[3,16,16,1024]{3,2,0,1:T(8,128)(2,1)}) %all-gather.2.cloned.1.call-update) | async-done | bytes 1572880 | tf_op jit(solution)/shard_map/all_gather | solution.py:94
  65.1 1.9 convert_element_type.275
  67.5 0.9 fusion.31
  68.4 0.7 fusion.56
  69.1 0.7 fusion.54
  69.8 0.7 fusion.52
  70.5 0.6 fusion.48
  71.1 0.7 fusion.46
  71.8 1.1 fusion.53
  72.9 1.0 fusion.47
  73.9 1.0 fusion.55
  75.0 1.1 fusion.49
  76.0 1.1 fusion.57
  77.3 1.0 fusion.44
  78.6 1.1 fusion.41
  79.7 1.9 copy.180
  81.6 1.9 copy.182
  83.5 0.9 maximum_bitcast_fusion.1
  84.3 0.7 pad_maximum_fusion.8
  85.0 1.7 copy.183
  86.7 1.8 copy.192
  88.5 0.8 copy.193
  89.8 1.6 collective-permute-start
  91.4 55.9 %all_gather.7 = bf16[1,2,6,16,256,3]{3,1,5,2,0,4:T(2,128)(2,1)} all-gather(bf16[1,2,6,16,16,3]{3,1,5,2,0,4:T(2,128)(2,1)} %copy.183), channel_id=1, replica_groups=mesh['tile'=16,'tf'=16] {'tile'}, dimensions={4}, use_global_device_ids=true | all-gather | bytes 313344 | tf_op jit(solution)/shard_map/all_gather | solution.py:117
  147.3 5.4 %copy.184 = bf16[1,2,6,16,256,3]{4,3,5,2,1,0:T(8,128)(2,1)S(1)} copy(bf16[1,2,6,16,256,3]{3,1,5,2,0,4:T(2,128)(2,1)} %all_gather.7) | data formatting | bytes 589824 | tf_op jit(solution)/shard_map/all_gather | solution.py:117
  153.1 0.7 slice.727
  153.9 0.6 copy-done.21
  154.9 1.1 copy.187
  156.0 4.3 %concatenate.289 = bf16[1,3,16,16,1030]{4,3,2,1,0:T(8,128)(2,1)} concatenate(bf16[1,3,16,16,3]{4,3,2,1,0:T(8,128)(2,1)S(1)} %copy.186, bf16[1,3,16,16,1024]{4,3,2,1,0:T(8,128)(2,1)} %copy-done.7, bf16[1,3,16,16,3]{4,3,2,1,0:T(8,128)(2,1)S(1)} %copy.187), dimensions={4} | concatenate | bytes 3164160 | tf_op jit(solution)/shard_map/concatenate | solution.py:130
  160.4 2.2 %slice_bitcast_fusion.4 = (bf16[1,16,16,1030]{3,2,0,1:T(8,128)(2,1)S(1)}, bf16[1,16,16,1030]{3,2,0,1:T(8,128)(2,1)}) fusion(bf16[1,3,16,16,1030]{4,3,2,1,0:T(8,128)(2,1)} %concatenate.289), kind=kLoop, calls=%fused_computation.72 | loop fusion | bytes 2109440 | tf_op jit(solution)/shard_map/squeeze | solution.py:140
  162.5 3.7 %subtract_bitcast_fusion.1 = f32[1,1,16,16,1024]{4,3,2,1,0:T(8,128)} fusion(bf16[1,16,16,1030]{3,2,0,1:T(8,128)(2,1)S(1)} %get-tuple-element.35, bf16[1,1,16,1024]{3,2,0,1:T(8,128)(2,1)} %get-tuple-element.68, bf16[1,15,16,1024]{3,2,0,1:T(8,128)(2,1)} %get-tuple-element.70, bf16[1,15,16,1024]{3,2,0,1:T(8,128)(2,1)} %get-tuple-element.69, ...), kind=kLoop, calls=%fused_computation.62 | loop fusion | flops 9175040 | bytes 7340032 | tf_op jit(solution)/shard_map/stack | solution.py:84
  166.2 1.4 fusion.50
  167.6 0.6 slice.577
  168.2 0.6 slice.580
  168.9 1.2 copy.189
  170.1 2.0 copy.188
  172.1 1.4 fusion.51
  173.6 1.3 copy.177
  174.9 1.2 copy.176
  176.1 0.8 maximum_bitcast_fusion
  177.1 2.5 %subtract_bitcast_fusion = f32[1,1,16,16,1024]{4,3,2,1,0:T(8,128)} fusion(bf16[1,16,22,1024]{3,2,0,1:T(8,128)(2,1)S(1)} %get-tuple-element.34, bf16[1,16,16,1030]{3,2,0,1:T(8,128)(2,1)S(1)} %copy-done.5), kind=kLoop, calls=%fused_computation.61 | loop fusion | flops 7602176 | bytes 7340032 | tf_op jit(solution)/shard_map/stack | solution.py:84
  179.7 2.1 subtract_bitcast_fusion.2
  181.8 13.7 %fusion.9 = f32[1,3,16,16,1024]{4,3,2,1,0:T(8,128)} fusion(f32[1,3,16,16,1024]{4,3,2,1,0:T(8,128)S(1)} %copy-done, f32[1,3,16,16,3]{4,3,2,1,0:T(8,128)S(1)} %copy.189, f32[1,3,16,16,3]{4,3,2,1,0:T(8,128)} %copy.188, f32[1,3,16,22,1024]{4,3,2,1,0:T(8,128)S(1)} %bitcast.80, f32[1,1,16,16,1024]{4,3,2,1,0:T(8,128)} %subtract_bitcast_fusion, ...), kind=kLoop, calls=%fused_computation.17 | loop fusion | flops 44040192 | bytes 50354176 | tf_op jit(solution)/shard_map/sub | solution.py:89
  195.5 2.6 %fusion.28 = f32[1,3,16,16,1024]{4,3,2,1,0:T(8,128)} fusion(f32[1,3,16,16,1024]{4,3,2,1,0:T(8,128)} %fusion.9, f32[1,3,16,16,1024]{4,3,2,1,0:T(8,128)S(1)} %copy-done), kind=kLoop, calls=%fused_computation.50 | loop fusion | flops 524288 | bytes 3145728 | tf_op jit(solution)/shard_map/scatter-add | solution.py:90
  198.0 6.1 %multiply_add_fusion = (f32[1,3,16,16,1024]{4,3,2,1,0:T(8,128)}, f32[1,3,16,16,1024]{4,3,2,1,0:T(8,128)}) fusion(f32[1,3,16,16,1024]{4,3,2,1,0:T(8,128)S(1)} %copy-done, f32[1,3,16,16,1024]{4,3,2,1,0:T(8,128)} %fusion.28, f32[1,3,16,16,1024]{4,3,2,1,0:T(8,128)S(1)} %copy-done.13), kind=kLoop, calls=%fused_computation.42 | loop fusion | flops 3932160 | bytes 15728640 | tf_op jit(solution)/shard_map/add | solution.py:154
  (80 shorter events, 2.6 us)
Async XLA Ops:
  7.2 8.6 %copy-start = (f32[1,3,16,16,1024]{4,3,2,1,0:T(8,128)S(1)}, f32[1,3,16,16,1024]{4,3,2,1,0:T(8,128)}, u32[]{:S(2)}) copy-start(f32[1,3,16,16,1024]{4,3,2,1,0:T(8,128)} %param.6) | copy-start | bytes 9437188
  7.2 58.0 %all-gather.2.cloned.1.call-start = ((), (), s32[]{:S(2)}) async-start(), calls=%async_computation | async-start | bytes 1671168 | tf_op jit(solution)/shard_map/all_gather | solution.py:94
  7.9 9.9 %copy-start.29 = (s32[2]{0:T(128)S(1)}, s32[2]{0:T(128)}, u32[]{:S(2)}) copy-start(s32[2]{0:T(128)} %param.9) | copy-start | bytes 28
  11.7 1.2 copy-start.8
  13.7 22.1 %collective-permute-start.2 = (bf16[1,3,16,3,1024]{4,2,3,1,0:T(8,128)(2,1)}, bf16[1,3,16,3,1024]{4,2,3,1,0:T(8,128)(2,1)}, u32[]{:S(2)}, u32[]{:S(2)}) collective-permute-start(bf16[1,3,16,3,1024]{4,2,3,1,0:T(8,128)(2,1)} %get-tuple-element.39), channel_id=1, source_target_pairs={{0,16},{16,32},{32,48},{48,64},{64,80},{80,96},{96,112},{112,128},... | collective-permute-start | bytes 884744 | tf_op jit(solution)/shard_map/ppermute | solution.py:23
  15.6 20.2 %collective-permute-start.3 = (bf16[1,3,16,3,1024]{4,2,3,1,0:T(8,128)(2,1)}, bf16[1,3,16,3,1024]{4,2,3,1,0:T(8,128)(2,1)}, u32[]{:S(2)}, u32[]{:S(2)}) collective-permute-start(bf16[1,3,16,3,1024]{4,2,3,1,0:T(8,128)(2,1)} %get-tuple-element.40), channel_id=1, source_target_pairs={{16,0},{32,16},{48,32},{64,48},{80,64},{96,80},{112,96},{128,112},... | collective-permute-start | bytes 884744 | tf_op jit(solution)/shard_map/ppermute | solution.py:24
  34.7 1.8 copy-start.9
  65.1 2.4 %copy-start.6 = (f32[1,3,16,16,1024]{4,3,2,1,0:T(8,128)S(1)}, f32[1,3,16,16,1024]{4,3,2,1,0:T(8,128)}, u32[]{:S(2)}) copy-start(f32[1,3,16,16,1024]{4,3,2,1,0:T(8,128)} %fusion.27) | copy-start | bytes 9437188
  68.4 8.7 %copy-start.1 = (bf16[1,16,16,1024]{3,2,0,1:T(8,128)(2,1)}, bf16[1,16,16,1024]{3,2,0,1:T(8,128)(2,1)S(1)}, u32[]{:S(2)}) copy-start(bf16[1,16,16,1024]{3,2,0,1:T(8,128)(2,1)S(1)} %get-tuple-element.18) | copy-start | bytes 1572868
  68.4 8.7 %copy-start.3 = (bf16[1,16,16,1024]{3,2,0,1:T(8,128)(2,1)}, bf16[1,16,16,1024]{3,2,0,1:T(8,128)(2,1)S(1)}, u32[]{:S(2)}) copy-start(bf16[1,16,16,1024]{3,2,0,1:T(8,128)(2,1)S(1)} %get-tuple-element.19) | copy-start | bytes 1572868
  68.4 8.7 %copy-start.10 = (bf16[1,1,16,16,1024]{4,3,2,1,0:T(8,128)(2,1)}, bf16[1,1,16,16,1024]{4,3,2,1,0:T(8,128)(2,1)S(1)}, u32[]{:S(2)}) copy-start(bf16[1,1,16,16,1024]{4,3,2,1,0:T(8,128)(2,1)S(1)} %get-tuple-element.20) | copy-start | bytes 1572868
  77.3 1.3 copy-start.7
  89.4 84.2 %collective-permute-start.1 = (bf16[1,3,16,3,1024]{4,2,3,1,0:T(8,128)(2,1)}, bf16[1,3,16,3,1024]{4,2,3,1,0:T(8,128)(2,1)}, u32[]{:S(2)}, u32[]{:S(2)}) collective-permute-start(bf16[1,3,16,3,1024]{4,2,3,1,0:T(8,128)(2,1)} %copy.193), channel_id=1, source_target_pairs={{16,0},{32,16},{48,32},{64,48},{80,64},{96,80},{112,96},{128,112},... | collective-permute-start | bytes 884744 | tf_op jit(solution)/shard_map/ppermute | solution.py:24
  89.8 85.0 %collective-permute-start = (bf16[1,3,16,3,1024]{4,2,3,1,0:T(8,128)(2,1)}, bf16[1,3,16,3,1024]{4,2,3,1,0:T(8,128)(2,1)}, u32[]{:S(2)}, u32[]{:S(2)}) collective-permute-start(bf16[1,3,16,3,1024]{4,2,3,1,0:T(8,128)(2,1)} %copy.192), channel_id=1, source_target_pairs={{0,16},{16,32},{32,48},{48,64},{64,80},{80,96},{96,112},{112,128},... | collective-permute-start | bytes 884744 | tf_op jit(solution)/shard_map/ppermute | solution.py:23
  153.1 0.8 copy-start.19
  153.8 0.7 copy-start.21
  162.5 5.1 %copy-start.20 = (f32[1,6,16,16,3]{3,2,4,1,0:T(8,128)S(1)}, f32[1,6,16,16,3]{3,2,4,1,0:T(8,128)}, u32[]{:S(2)}) copy-start(f32[1,6,16,16,3]{3,2,4,1,0:T(8,128)} %copy-done.19) | copy-start | bytes 55300
  162.5 5.7 %copy-start.22 = (f32[1,6,16,16,3]{3,2,4,1,0:T(8,128)S(1)}, f32[1,6,16,16,3]{3,2,4,1,0:T(8,128)}, u32[]{:S(2)}) copy-start(f32[1,6,16,16,3]{3,2,4,1,0:T(8,128)} %copy-done.21) | copy-start | bytes 55300
  172.1 3.9 %copy-start.2 = (bf16[1,16,16,1024]{3,2,0,1:T(8,128)(2,1)S(1)}, bf16[1,16,16,1024]{3,2,0,1:T(8,128)(2,1)}, u32[]{:S(2)}) copy-start(bf16[1,16,16,1024]{3,2,0,1:T(8,128)(2,1)} %copy-done.1) | copy-start | bytes 1572868
  172.1 3.9 %copy-start.4 = (bf16[1,16,16,1024]{3,2,0,1:T(8,128)(2,1)S(1)}, bf16[1,16,16,1024]{3,2,0,1:T(8,128)(2,1)}, u32[]{:S(2)}) copy-start(bf16[1,16,16,1024]{3,2,0,1:T(8,128)(2,1)} %copy-done.3) | copy-start | bytes 1572868
  172.1 4.0 %copy-start.11 = (bf16[1,1,16,16,1024]{4,3,2,1,0:T(8,128)(2,1)S(1)}, bf16[1,1,16,16,1024]{4,3,2,1,0:T(8,128)(2,1)}, u32[]{:S(2)}) copy-start(bf16[1,1,16,16,1024]{4,3,2,1,0:T(8,128)(2,1)} %copy-done.10) | copy-start | bytes 1572868
  173.5 3.4 %copy-start.5 = (bf16[1,16,16,1030]{3,2,0,1:T(8,128)(2,1)S(1)}, bf16[1,16,16,1030]{3,2,0,1:T(8,128)(2,1)}, u32[]{:S(2)}) copy-start(bf16[1,16,16,1030]{3,2,0,1:T(8,128)(2,1)} %get-tuple-element.36) | copy-start | bytes 1582084
  176.1 5.6 %slice-start = ((s8[4718592]{0:T(1024)(128)(4,1)}), s8[4194304]{0:T(1024)(128)(4,1)S(1)}, s32[]{:S(2)}) async-start(s8[4718592]{0:T(1024)(128)(4,1)} %bitcast.79), calls=%async_computation.1 | async-start | bytes 8388608
  176.9 2.6 %copy-start.15 = (bf16[1,14,16,1024]{3,2,0,1:T(8,128)(2,1)S(1)}, bf16[1,14,16,1024]{3,2,0,1:T(8,128)(2,1)}, u32[]{:S(2)}) copy-start(bf16[1,14,16,1024]{3,2,0,1:T(8,128)(2,1)} %get-tuple-element.53) | copy-start | bytes 1376260
  177.0 2.6 %copy-start.16 = (bf16[1,14,16,1024]{3,2,0,1:T(8,128)(2,1)S(1)}, bf16[1,14,16,1024]{3,2,0,1:T(8,128)(2,1)}, u32[]{:S(2)}) copy-start(bf16[1,14,16,1024]{3,2,0,1:T(8,128)(2,1)} %get-tuple-element.54) | copy-start | bytes 1376260
  177.0 2.6 %copy-start.17 = (bf16[1,13,16,1024]{3,2,0,1:T(8,128)(2,1)S(1)}, bf16[1,13,16,1024]{3,2,0,1:T(8,128)(2,1)}, u32[]{:S(2)}) copy-start(bf16[1,13,16,1024]{3,2,0,1:T(8,128)(2,1)} %get-tuple-element.49) | copy-start | bytes 1277956
  177.0 2.6 %copy-start.18 = (bf16[1,13,16,1024]{3,2,0,1:T(8,128)(2,1)S(1)}, bf16[1,13,16,1024]{3,2,0,1:T(8,128)(2,1)}, u32[]{:S(2)}) copy-start(bf16[1,13,16,1024]{3,2,0,1:T(8,128)(2,1)} %get-tuple-element.50) | copy-start | bytes 1277956
  177.0 2.6 %copy-start.23 = (bf16[1,3,16,1024]{3,2,0,1:T(8,128)(2,1)S(1)}, bf16[1,3,16,1024]{3,2,0,1:T(8,128)(2,1)}, u32[]{:S(2)}) copy-start(bf16[1,3,16,1024]{3,2,0,1:T(8,128)(2,1)} %get-tuple-element.47) | copy-start | bytes 294916
  177.0 2.6 %copy-start.24 = (bf16[1,3,16,1024]{3,2,0,1:T(8,128)(2,1)S(1)}, bf16[1,3,16,1024]{3,2,0,1:T(8,128)(2,1)}, u32[]{:S(2)}) copy-start(bf16[1,3,16,1024]{3,2,0,1:T(8,128)(2,1)} %get-tuple-element.48) | copy-start | bytes 294916
  177.0 2.6 %copy-start.25 = (bf16[1,2,16,1024]{3,2,0,1:T(8,128)(2,1)S(1)}, bf16[1,2,16,1024]{3,2,0,1:T(8,128)(2,1)}, u32[]{:S(2)}) copy-start(bf16[1,2,16,1024]{3,2,0,1:T(8,128)(2,1)} %get-tuple-element.51) | copy-start | bytes 196612
  177.0 2.6 %copy-start.26 = (bf16[1,2,16,1024]{3,2,0,1:T(8,128)(2,1)S(1)}, bf16[1,2,16,1024]{3,2,0,1:T(8,128)(2,1)}, u32[]{:S(2)}) copy-start(bf16[1,2,16,1024]{3,2,0,1:T(8,128)(2,1)} %get-tuple-element.52) | copy-start | bytes 196612
  177.0 2.6 %copy-start.27 = (bf16[1,1,16,1024]{3,2,0,1:T(8,128)(2,1)S(1)}, bf16[1,1,16,1024]{3,2,0,1:T(8,128)(2,1)}, u32[]{:S(2)}) copy-start(bf16[1,1,16,1024]{3,2,0,1:T(8,128)(2,1)} %get-tuple-element.55) | copy-start | bytes 98308
  177.0 2.6 %copy-start.28 = (bf16[1,1,16,1024]{3,2,0,1:T(8,128)(2,1)S(1)}, bf16[1,1,16,1024]{3,2,0,1:T(8,128)(2,1)}, u32[]{:S(2)}) copy-start(bf16[1,1,16,1024]{3,2,0,1:T(8,128)(2,1)} %get-tuple-element.56) | copy-start | bytes 98308
  177.0 4.7 %slice-start.1 = ((s8[4718592]{0:T(1024)(128)(4,1)}), s8[524288]{0:T(1024)(128)(4,1)S(1)}, s32[]{:S(2)}) async-start(s8[4718592]{0:T(1024)(128)(4,1)} %bitcast.79), calls=%async_computation.2 | async-start | bytes 1048576
  179.6 2.1 %copy-start.12 = (f32[1,1,16,16,1024]{4,3,2,1,0:T(8,128)S(1)}, f32[1,1,16,16,1024]{4,3,2,1,0:T(8,128)}, u32[]{:S(2)}) copy-start(f32[1,1,16,16,1024]{4,3,2,1,0:T(8,128)} %subtract_bitcast_fusion.1) | copy-start | bytes 3145732
  179.6 2.1 %copy-start.14 = (f32[1,3,3,16,1024]{4,3,2,1,0:T(8,128)S(1)}, f32[1,3,3,16,1024]{4,3,2,1,0:T(8,128)}, u32[]{:S(2)}) copy-start(f32[1,3,3,16,1024]{4,3,2,1,0:T(8,128)} %get-tuple-element.21) | copy-start | bytes 1769476
  195.4 2.6 %copy-start.13 = (f32[1,3,16,16,1024]{4,3,2,1,0:T(8,128)S(1)}, f32[1,3,16,16,1024]{4,3,2,1,0:T(8,128)}, u32[]{:S(2)}) copy-start(f32[1,3,16,16,1024]{4,3,2,1,0:T(8,128)} %param.7) | copy-start | bytes 9437188
Sparse Core Ops, SparseCore 0:
  10.7 54.3 all-gather.1
where the time goes:
time: 212 us; the launch traced here: 211 us
  local copies, waits for them, and re-layouts  67.8 us (32%)
  blocking collectives  55.9 us (26%)
  other arithmetic  42.9 us (20%)
  waiting for transfers between devices  24.5 us (12%)
  between operations  15.8 us (7%)
  starting transfers between devices  4.09 us (2%)
    all_gather x1, blocking collectives, body(): lax.all_gather(strips.astype(jnp.bfloat16), 'tile', axis=4, tiled=True)  55.9 us
    slice x18, local copies, waits for them, and re-layouts, view(): jnp.roll(arrays[name][:, channel], -offset, axis=-3).astype(jnp.float32)  24.3 us
    all_gather x1, waiting for transfers between devices, make_emf(): whole_velocity = lax.all_gather(velocity, 'tf', axis=1, tiled=True)  23.8 us
    sub x1, other arithmetic, tendency(): rate = curl + DIFFUSIVITY * laplace - sweep * field_dy  13.7 us
    unnamed x67, local copies, waits for them, and re-layouts  9.79 us
    another operation x3, other arithmetic, tendency(): curl = jnp.stack([curl_x, curl_y, curl_z], 1)  8.25 us
    add x1, other arithmetic, body(): new_field = test_field + RK_BETA * new_register  6.1 us
    all_gather x1, local copies, waits for them, and re-layouts, body(): lax.all_gather(strips.astype(jnp.bfloat16), 'tile', axis=4, tiled=True)  5.4 us
  transfers between devices with their start and end apart: 5, of which 1 were waited for; matrix products, arithmetic and copies ran while one was open for 26% of the time, Pallas kernels for 0%

commit v1 on v0

v1 whole, which is shorter than its diff:
```python
import functools
import math

import jax
import jax.numpy as jnp
import ml_dtypes
import numpy as np
from jax import lax
from jax.experimental import pallas as pl
from jax.experimental.pallas import tpu as pltpu
from jax.sharding import PartitionSpec as P

BF = jnp.bfloat16
F32 = jnp.float32
TIME_STEP = 0.3
RK_ALPHA = -5.0 / 9.0
RK_BETA = 15.0 / 16.0
SWEEP_SPEED = 0.75
STRETCH_RATE = 0.375
SCALE = TIME_STEP / 60.0

FIRST = {-3: -1, -2: 9, -1: -45, 1: 45, 2: -9, 3: 1}
SECOND = {-3: 2, -2: -27, -1: 270, 0: -490, 1: 270, 2: -27, 3: 2}

NZ, ROWS, NX = 16, 16, 1024
CELLS = NZ * ROWS
BLOCK = 256
BLOCKS = NX // BLOCK
ORDER = (0, 3, 1, 2)
HALO = 3 * NZ


def band(coefs):
    out = np.zeros((BLOCK, BLOCK))
    for offset, value in coefs.items():
        for x in range(BLOCK):
            if 0 <= x + offset < BLOCK:
                out[x + offset, x] = value
    return out


def band_edges(coefs):
    out = np.zeros((256, BLOCK))
    for offset, value in coefs.items():
        for x in range(BLOCK):
            if x + offset < 0:
                out[128 + x + offset, x] = value
            elif x + offset >= BLOCK:
                out[128 + x + offset - BLOCK, x] = value
    return out


def rows_y(coefs):
    out = np.zeros((CELLS, CELLS))
    for offset, value in coefs.items():
        for y in range(ROWS):
            if 0 <= y + offset < ROWS:
                for z in range(NZ):
                    out[z * ROWS + y, z * ROWS + y + offset] += value
    return out


def rows_z(coefs):
    out = np.zeros((CELLS, CELLS))
    for offset, value in coefs.items():
        for z in range(NZ):
            for y in range(ROWS):
                out[z * ROWS + y, (z + offset) % NZ * ROWS + y] += value
    return out


def rows_out(coefs):
    out = np.zeros((2, 3, NZ, CELLS))
    for z in range(NZ):
        for j in range(3):
            for s in range(3):
                low, high = s - 3 - j, 3 + s - j
                if low in coefs and low >= -3:
                    out[0, j, z, z * ROWS + ROWS - 3 + s] = coefs[low]
                if high <= 3:
                    out[1, j, z, z * ROWS + s] = coefs[high]
    return out.reshape(2 * HALO, CELLS)


def strip_out(coefs):
    out = np.zeros((256, 128))
    for group in range(16):
        for cell in range(3):
            for s in range(3):
                low, high = s - 3 - cell, 3 + s - cell
                if low >= -3:
                    out[253 + s, group * 8 + cell] = coefs[low]
                if high <= 3:
                    out[s, group * 8 + 4 + cell] = coefs[high]
    return out


def halo_in():
    out = np.zeros((CELLS, 2, 3, NZ))
    for z in range(NZ):
        for j in range(3):
            out[z * ROWS + j, 0, j, z] = 1
            out[z * ROWS + ROWS - 3 + j, 1, j, z] = 1
    return out.reshape(CELLS, 2 * HALO)


def strip_in():
    out = np.zeros((BLOCKS, 128, BLOCK))
    for lane in range(128):
        cell = lane % 4
        if cell < 3:
            if lane % 8 < 4:
                out[0, lane, cell] = 1
            else:
                out[BLOCKS - 1, lane, BLOCK - 3 + cell] = 1
    return out


def small(array):
    return jnp.asarray(np.asarray(array).astype(ml_dtypes.bfloat16))


def profiles():
    z = np.arange(NZ, dtype=np.float32)
    out = np.zeros((16, 2, NZ), np.float32)
    for k in range(16):
        phase = np.float32(2.0 * math.pi) * np.float32(k // 4 + 1) * z / np.float32(NZ)
        out[k, k % 2] = np.cos(phase) if k // 2 % 2 == 0 else np.sin(phase)
    return out.reshape(-1)


def dot(a, b):
    return jnp.dot(a, b, preferred_element_type=F32)


def exchange(
    tiles, profile, field_hbm, register_hbm, velocity_hbm, zy_hbm, out_hbm, x_hbm, edge_hbm, strip_hbm,
    base, halo, strips,
    field, register, vel, work, sums, zy, outw, xw, edgew, stripw,
    load_sem, const_sem, vsend, vrecv, hsend, hrecv, ssend, srecv,
):
    t = lax.axis_index("tile")
    k = lax.axis_index("tf")
    xi, hc = k // 4, k % 4
    core = k % 2
    plus, minus = (xi + 1) % 4, (xi + 3) % 4
    opposite = (xi + 2) % 4
    other = hc + 2 - (hc // 2) * 4
    at_plus, at_minus = plus * 4 + hc, minus * 4 + hc
    partner = xi * 4 + other
    sibling = k + 1 - 2 * core

    own_velocity = pltpu.make_async_copy(velocity_hbm.at[:, 0], vel.at[k], load_sem.at[0])
    own_velocity.start()
    load_field = pltpu.make_async_copy(field_hbm, field, load_sem.at[1])
    load_field.start()
    pairs = ((zy_hbm, zy), (out_hbm, outw), (x_hbm, xw), (edge_hbm, edgew), (strip_hbm, stripw))
    consts = [pltpu.make_async_copy(a, b, const_sem.at[i]) for i, (a, b) in enumerate(pairs)]
    for copy in consts:
        copy.start()
    load_register = pltpu.make_async_copy(register_hbm, register, load_sem.at[2])
    load_register.start()

    barrier = pltpu.get_barrier_semaphore()
    for peer in (at_plus, at_minus, partner, sibling):
        pl.semaphore_signal(barrier, inc=1, device_id={"tf": peer})
    for step in range(1, tiles):
        pl.semaphore_signal(barrier, inc=1, device_id={"tile": (t + step) % tiles})
    pl.semaphore_wait(barrier, 4 + tiles - 1)

    started = []

    def lanes(part):
        return pl.ds(ORDER[part] * BLOCK, BLOCK)

    def plane_copy(plane, part, kind, peer):
        block = vel.at[plane, :, :, lanes(part)]
        return pltpu.make_async_remote_copy(
            src_ref=block,
            dst_ref=block,
            send_sem=vsend.at[part, kind],
            recv_sem=vrecv.at[part, plane],
            device_id={"tf": peer},
        )

    def send(plane, part, kind, peer):
        copy = plane_copy(plane, part, kind, peer)
        copy.start()
        started.append(copy)

    def arrived(plane, part):
        plane_copy(plane, part, 0, sibling).wait_recv()

    def of(x, h):
        return x * 4 + h

    own_velocity.wait()
    for part in range(BLOCKS):
        send(k, part, 0, partner)
        send(k, part, 1, at_plus)
        send(k, part, 2, at_minus)
        send(k, part, 3, sibling)
    for part in range(BLOCKS):
        arrived(partner, part)
        send(partner, part, 4, at_plus)
        send(partner, part, 5, at_minus)
        send(partner, part, 6, sibling)

    def forward(part):
        arrived(of(minus, hc), part)
        send(of(minus, hc), part, 7, at_plus)
        send(of(minus, hc), part, 8, sibling)
        arrived(of(plus, hc), part)
        send(of(plus, hc), part, 9, sibling)
        arrived(of(plus, other), part)
        send(of(plus, other), part, 10, at_minus)
        send(of(plus, other), part, 11, sibling)
        arrived(of(minus, other), part)
        send(of(minus, other), part, 12, sibling)

    def last_forward(part):
        arrived(of(opposite, hc), part)
        send(of(opposite, hc), part, 13, sibling)
        arrived(of(opposite, other), part)
        send(of(opposite, other), part, 14, sibling)

    def from_sibling(part):
        flip = 1 - 2 * core
        for x in range(4):
            for h in range(2):
                arrived(x * 4 + h * 2 + core + flip, part)

    def emf_of(part):
        block = lanes(part)
        xpos = (lax.broadcasted_iota(jnp.int32, (ROWS, BLOCK), 1) + ORDER[part] * BLOCK).astype(F32)
        sweep = -SWEEP_SPEED * (2.0 * xpos / (NX - 1) - 1.0)

        def plane(z, carry):
            rows = pl.ds(pl.multiple_of(z * ROWS, ROWS), ROWS)
            f = [field[c, rows, block] for c in range(3)]
            v = [vel[z, c, :, block].astype(F32) for c in range(3)]
            summed = [
                (f[0] + profile[k * 32 + z]).astype(BF).astype(F32),
                (f[1] + profile[k * 32 + 16 + z]).astype(BF).astype(F32),
                f[2].astype(BF).astype(F32),
            ]
            emf_x = v[1] * summed[2] - v[2] * summed[1]
            emf_y = v[2] * summed[0] - v[0] * summed[2]
            emf_z = v[0] * summed[1] - v[1] * summed[0]
            mixed = (emf_z - sweep * f[0], -(sweep * f[1]), -emf_x - sweep * f[2])
            for c, value in enumerate((-emf_y, emf_x, emf_z)):
                work[c, rows, block] = value.astype(BF)
            for c in range(3):
                work[c, pl.ds(pl.multiple_of(CELLS + z * ROWS, ROWS), ROWS), block] = mixed[c].astype(BF)
                work[c, pl.ds(pl.multiple_of(2 * CELLS + z * ROWS, ROWS), ROWS), block] = (f[c] * (1.0 / 30.0)).astype(BF)
            return carry

        lax.fori_loop(0, NZ, plane, 0)

    def halo_copies(part):
        block = lanes(part)
        out = []
        for side, peer in ((0, (t + 1) % tiles), (1, (t + tiles - 1) % tiles)):
            out.append(
                pltpu.make_async_remote_copy(
                    src_ref=sums.at[:, side, :, block],
                    dst_ref=halo.at[:, side, :, block],
                    send_sem=hsend.at[side, part],
                    recv_sem=hrecv.at[side, part],
                    device_id={"tile": peer},
                )
            )
        return out

    def halo_of(part):
        block = lanes(part)
        for c in range(3):
            total = dot(outw[...], work[c, CELLS:, block]).astype(BF)
            for side in range(2):
                sums[c, side, :, block] = total[side * HALO : (side + 1) * HALO]
        for copy in halo_copies(part):
            copy.start()
            started.append(copy)

    def strip_copy(step, at):
        return pltpu.make_async_remote_copy(
            src_ref=strips.at[:, pl.ds(pl.multiple_of(at * ROWS, ROWS), ROWS), :],
            dst_ref=strips.at[:, pl.ds(pl.multiple_of(at * ROWS, ROWS), ROWS), :],
            send_sem=ssend.at[step],
            recv_sem=srecv.at[at],
            device_id={"tile": (t + step) % tiles},
        )

    def strips_of():
        row = lax.broadcasted_iota(jnp.int32, (CELLS, 128), 0)
        lane = lax.broadcasted_iota(jnp.int32, (CELLS, 128), 1)
        own = (row // ROWS) == (lane // 8)

        def ends(c, part):
            rows = slice(part * CELLS, (part + 1) * CELLS)
            return jnp.concatenate([work[c, rows, :128], work[c, rows, NX - 128 :]], axis=1)

        for c in range(3):
            total = dot(ends(c, 2), stripw[:256])
            if c == 1:
                total += dot(ends(2, 0), stripw[256:])
            if c == 2:
                total += dot(ends(0, 0), stripw[256:])
            packed = jnp.sum(jnp.where(own, total, 0.0).reshape(NZ, ROWS, 128), axis=0)
            strips[c, pl.ds(pl.multiple_of(t * ROWS, ROWS), ROWS), :] = packed.astype(BF)
        for step in range(1, tiles):
            copy = strip_copy(step, t)
            copy.start()
            started.append(copy)

    forward(0)
    load_field.wait()
    for copy in consts:
        copy.wait()
    for part in range(BLOCKS):
        last_forward(part)
        if part + 1 < BLOCKS:
            forward(part + 1)
        from_sibling(part)
        emf_of(part)
        halo_of(part)
        if part == 1:
            strips_of()

    load_register.wait()
    for b in range(BLOCKS):
        block = slice(b * BLOCK, (b + 1) * BLOCK)

        def ends(c, part):
            rows = slice(part * CELLS, (part + 1) * CELLS)
            before = work[c, rows, b * BLOCK - 128 : b * BLOCK] if b > 0 else None
            after = work[c, rows, (b + 1) * BLOCK : (b + 1) * BLOCK + 128] if b + 1 < BLOCKS else None
            if before is None:
                return after, slice(128, 256)
            if after is None:
                return before, slice(0, 128)
            return jnp.concatenate([before, after], axis=1), slice(0, 256)

        for c in range(3):
            if c < 2:
                total = dot(zy[...], work[c, :, block])
            else:
                total = dot(zy[:, CELLS:], work[c, CELLS:, block])
            total += dot(work[c, 2 * CELLS :, block], xw[:256])
            far, near = ends(c, 2)
            total += dot(far, edgew[:256][near])
            if c > 0:
                source = 2 if c == 1 else 0
                total += dot(work[source, :CELLS, block], xw[256:])
                far, near = ends(source, 0)
                total += dot(far, edgew[256:][near])
            result = RK_ALPHA * register[c, :, block] + SCALE * total
            if c == 1:
                result -= TIME_STEP * STRETCH_RATE * field[0, :, block]
            base[c, :, block] = result

    for part in range(BLOCKS):
        for copy in halo_copies(part):
            copy.wait_recv()
    for step in range(1, tiles):
        strip_copy(step, (t + step) % tiles).wait_recv()
    for copy in started:
        copy.wait_send()


def finish(shift, field, base, halo, strips, spread, ends, new_field, new_register, ghost):
    @pl.when(pl.program_id(0) == 0)
    def _():
        t = lax.axis_index("tile")
        total = strips.shape[1]
        place = lax.broadcasted_iota(jnp.int32, (ROWS, total), 0) + t * ROWS
        source = lax.broadcasted_iota(jnp.int32, (ROWS, total), 1)
        lane = lax.broadcasted_iota(jnp.int32, (ROWS, 128), 1)
        picks = [jnp.where((place + shift[side]) % total == source, 1.0, 0.0).astype(BF) for side in range(2)]
        for c in range(3):
            low, high = (dot(pick, strips[c]) for pick in picks)
            both = jnp.where(lane % 8 < 4, low, high)
            for z in range(NZ):
                ghost[c, z * ROWS : (z + 1) * ROWS] = jnp.where(lane // 8 == z, both, 0.0).astype(BF)

    for c in range(3):
        total = dot(spread[...], halo[c].reshape(2 * HALO, BLOCK)) + dot(ghost[c], ends[0])
        register = base[c] + SCALE * total
        new_register[c] = register
        new_field[c] = field[c] + RK_BETA * register


def body(tiles, test_field, register, velocity, shear_shift):
    field = test_field.reshape(3, CELLS, NX)
    reg = register.reshape(3, CELLS, NX)
    zy = small(np.concatenate([rows_z(FIRST), rows_y(FIRST), rows_y(SECOND) + rows_z(SECOND)], 1))
    outw = small(np.concatenate([rows_out(FIRST), rows_out(SECOND)], 1))
    xw = small(np.concatenate([band(SECOND), -band(FIRST)], 0))
    edgew = small(np.concatenate([band_edges(SECOND), -band_edges(FIRST)], 0))
    stripw = small(np.concatenate([strip_out(SECOND), -strip_out(FIRST)], 0))
    anywhere = pl.BlockSpec(memory_space=pl.ANY)
    vmem = pl.BlockSpec(memory_space=pltpu.VMEM)
    dma = pltpu.SemaphoreType.DMA
    base, halo, strips = pl.pallas_call(
        functools.partial(exchange, tiles),
        out_shape=(
            jax.ShapeDtypeStruct((3, CELLS, NX), F32),
            jax.ShapeDtypeStruct((3, 2, HALO, NX), BF),
            jax.ShapeDtypeStruct((3, tiles * ROWS, 128), BF),
        ),
        in_specs=[pl.BlockSpec(memory_space=pltpu.SMEM)] + [anywhere] * 8,
        out_specs=(vmem, vmem, vmem),
        scratch_shapes=[
            pltpu.VMEM((3, CELLS, NX), F32),
            pltpu.VMEM((3, CELLS, NX), F32),
            pltpu.VMEM((16, 3, ROWS, NX), BF),
            pltpu.VMEM((3, 3 * CELLS, NX), BF),
            pltpu.VMEM((3, 2, HALO, NX), BF),
            pltpu.VMEM(zy.shape, BF),
            pltpu.VMEM(outw.shape, BF),
            pltpu.VMEM(xw.shape, BF),
            pltpu.VMEM(edgew.shape, BF),
            pltpu.VMEM(stripw.shape, BF),
            dma((3,)),
            dma((5,)),
            dma((BLOCKS, 15)),
            dma((BLOCKS, 16)),
            dma((2, BLOCKS)),
            dma((2, BLOCKS)),
            dma((tiles,)),
            dma((tiles,)),
        ],
        compiler_params=pltpu.CompilerParams(
            collective_id=0, has_side_effects=True, vmem_limit_bytes=40 * 2**20
        ),
        name="exchange",
    )(jnp.asarray(profiles()), field, reg, velocity, zy, outw, xw, edgew, stripw)

    spread, ends = small(halo_in()), small(strip_in())
    whole = pl.BlockSpec((3, CELLS, BLOCK), lambda b: (0, 0, b))
    new_field, new_register = pl.pallas_call(
        finish,
        grid=(BLOCKS,),
        out_shape=(jax.ShapeDtypeStruct((3, CELLS, NX), F32),) * 2,
        in_specs=[
            pl.BlockSpec(memory_space=pltpu.SMEM),
            whole,
            whole,
            pl.BlockSpec((3, 2, HALO, BLOCK), lambda b: (0, 0, 0, b)),
            pl.BlockSpec((3, tiles * ROWS, 128), lambda b: (0, 0, 0)),
            pl.BlockSpec((CELLS, 2 * HALO), lambda b: (0, 0)),
            pl.BlockSpec((1, 128, BLOCK), lambda b: (b, 0, 0)),
        ],
        out_specs=(whole, whole),
        scratch_shapes=[pltpu.VMEM((3, CELLS, 128), BF)],
        compiler_params=pltpu.CompilerParams(vmem_limit_bytes=24 * 2**20),
        name="finish",
    )(shear_shift, field, base, halo, strips, spread, ends)
    return new_field.reshape(test_field.shape), new_register.reshape(register.shape)


def solution(mesh):
    cells = P("tf", None, None, "tile", None)
    return jax.shard_map(
        functools.partial(body, mesh.shape["tile"]),
        mesh=mesh,
        in_specs=(cells, cells, P(None, "tf", "tile", None), P()),
        out_specs=(cells, cells),
        check_vma=False,
    )
```

time: 212 us -> 55.5 us (0.26)
  the two profiles are of different devices: /device:TPU:32 before, /device:TPU:1 now
where the time goes in v1:
time: 55.5 us; the launch traced here: 55.1 us
  Pallas kernels  44.4 us (80%)
  local copies, waits for them, and re-layouts  10 us (18%)
  between operations  0.68 us (1%)
    pallas_call x1, Pallas kernels, body(): pl.pallas_call(functools.partial(exchange, tiles), out_shape=(jax.ShapeDt...  39.8 us
    unnamed x24, local copies, waits for them, and re-layouts  10 us
    pallas_call x1, Pallas kernels, body(): pl.pallas_call(finish, grid=(BLOCKS,), out_shape=(jax.ShapeDtypeStruct((3...  4.58 us

profile of v1, /device:TPU:1, one launch (start us, length us, event | category | flops | bytes accessed | tf_op | source)
XLA Modules:
  0.0 55.1 jit_solution(6164068598949487585)
XLA Ops:
  0.6 0.0 copy-start
  0.6 1.9 %copy-done = f32[1,3,16,16,1024]{4,3,2,1,0:T(8,128)S(1)} copy-done((f32[1,3,16,16,1024]{4,3,2,1,0:T(8,128)S(1)}, f32[1,3,16,16,1024]{4,3,2,1,0:T(8,128)}, u32[]{:S(2)}) %copy-start) | copy-done | bytes 3145752
  2.5 0.0 copy-start.1
  2.5 1.9 %copy-done.1 = f32[1,3,16,16,1024]{4,3,2,1,0:T(8,128)S(1)} copy-done((f32[1,3,16,16,1024]{4,3,2,1,0:T(8,128)S(1)}, f32[1,3,16,16,1024]{4,3,2,1,0:T(8,128)}, u32[]{:S(2)}) %copy-start.1) | copy-done | bytes 3145752
  4.4 0.0 copy-start.2
  4.4 1.0 %copy-done.2 = bf16[256,768]{1,0:T(8,128)(2,1)S(1)} copy-done((bf16[256,768]{1,0:T(8,128)(2,1)S(1)}, bf16[256,768]{1,0:T(8,128)(2,1)}, u32[]{:S(2)}) %copy-start.2) | copy-done | bytes 393240
  5.4 0.0 copy-start.3
  5.4 0.9 %copy-done.3 = bf16[512,256]{1,0:T(8,128)(2,1)S(1)} copy-done((bf16[512,256]{1,0:T(8,128)(2,1)S(1)}, bf16[512,256]{1,0:T(8,128)(2,1)}, u32[]{:S(2)}) %copy-start.3) | copy-done | bytes 262168
  6.4 0.0 copy-start.4
  6.4 0.9 %copy-done.4 = bf16[512,256]{1,0:T(8,128)(2,1)S(1)} copy-done((bf16[512,256]{1,0:T(8,128)(2,1)S(1)}, bf16[512,256]{1,0:T(8,128)(2,1)}, u32[]{:S(2)}) %copy-start.4) | copy-done | bytes 262168
  7.3 0.0 copy-start.6
  7.3 0.9 %copy-done.6 = bf16[512,128]{1,0:T(8,128)(2,1)S(1)} copy-done((bf16[512,128]{1,0:T(8,128)(2,1)S(1)}, bf16[512,128]{1,0:T(8,128)(2,1)}, u32[]{:S(2)}) %copy-start.6) | copy-done | bytes 131096
  8.2 0.0 copy-start.7
  8.2 0.9 %copy-done.7 = bf16[3,1,16,1024]{3,2,1,0:T(8,128)(2,1)S(1)} copy-done((bf16[3,1,16,1024]{3,2,1,0:T(8,128)(2,1)S(1)}, bf16[3,1,16,1024]{3,2,1,0:T(8,128)(2,1)}, u32[]{:S(2)}) %copy-start.7) | copy-done | bytes 98328
  9.1 0.0 copy-start.8
  9.1 0.9 %copy-done.8 = bf16[96,512]{1,0:T(8,128)(2,1)S(1)} copy-done((bf16[96,512]{1,0:T(8,128)(2,1)S(1)}, bf16[96,512]{1,0:T(8,128)(2,1)}, u32[]{:S(2)}) %copy-start.8) | copy-done | bytes 98328
  10.0 0.0 copy-start.10
  10.0 0.7 %copy-done.10 = f32[512]{0:T(512)S(1)} copy-done((f32[512]{0:T(512)S(1)}, f32[512]{0:T(512)}, u32[]{:S(2)}) %copy-start.10) | copy-done | bytes 2072
  10.7 0.0 copy-start.5
  10.7 0.0 copy-start.9
  10.7 0.0 copy-start.11
  10.7 39.8 %exchange.1 = (f32[3,256,1024]{2,1,0:T(8,128)S(1)}, bf16[3,2,48,1024]{3,2,1,0:T(8,128)(2,1)S(1)}, bf16[3,256,128]{2,1,0:T(8,128)(2,1)S(1)}) custom-call(f32[512]{0:T(512)S(1)} %copy-done.10, f32[3,256,1024]{2,1,0:T(8,128)S(1)} %bitcast.4, f32[3,256,1024]{2,1,0:T(8,128)S(1)} %bitcast.6, bf16[3,1,16,1024]{3,2,1,0:T(8,128)(2,1)S(1)} %copy-done.7, ...), custom_call_target="tpu_custom_call" | custom-call | tf_op jit(solution)/shard_map/exchange/pallas_call | solution.py:404
  50.5 0.0 copy-done.5
  50.5 0.0 copy-done.9
  50.5 0.0 copy-done.11
  50.6 4.6 %finish.1 = (f32[3,256,1024]{2,1,0:T(8,128)}, f32[3,256,1024]{2,1,0:T(8,128)}) custom-call(s32[2]{0:T(128)S(1)} %copy-done.11, f32[3,256,1024]{2,1,0:T(8,128)S(1)} %bitcast.5, f32[3,256,1024]{2,1,0:T(8,128)S(1)} %get-tuple-element.7.base, bf16[3,2,48,1024]{3,2,1,0:T(8,128)(2,1)S(1)} %get-tuple-element.8.halo, ...), custom_call_target="tpu_custom_call" | custom-call | tf_op jit(solution)/shard_map/finish/pallas_call | solution.py:441
Async XLA Ops:
  0.6 1.9 %copy-start = (f32[1,3,16,16,1024]{4,3,2,1,0:T(8,128)S(1)}, f32[1,3,16,16,1024]{4,3,2,1,0:T(8,128)}, u32[]{:S(2)}) copy-start(f32[1,3,16,16,1024]{4,3,2,1,0:T(8,128)} %param.12) | copy-start | bytes 9437188
  2.5 1.9 %copy-start.1 = (f32[1,3,16,16,1024]{4,3,2,1,0:T(8,128)S(1)}, f32[1,3,16,16,1024]{4,3,2,1,0:T(8,128)}, u32[]{:S(2)}) copy-start(f32[1,3,16,16,1024]{4,3,2,1,0:T(8,128)} %param.13) | copy-start | bytes 9437188
  4.4 1.0 %copy-start.2 = (bf16[256,768]{1,0:T(8,128)(2,1)S(1)}, bf16[256,768]{1,0:T(8,128)(2,1)}, u32[]{:S(2)}) copy-start(bf16[256,768]{1,0:T(8,128)(2,1)} %constant.16.clone.zy_hbm) | copy-start | bytes 1179652
  5.4 0.9 %copy-start.3 = (bf16[512,256]{1,0:T(8,128)(2,1)S(1)}, bf16[512,256]{1,0:T(8,128)(2,1)}, u32[]{:S(2)}) copy-start(bf16[512,256]{1,0:T(8,128)(2,1)} %constant.19.clone.edge_hbm) | copy-start | bytes 786436
  6.4 0.9 %copy-start.4 = (bf16[512,256]{1,0:T(8,128)(2,1)S(1)}, bf16[512,256]{1,0:T(8,128)(2,1)}, u32[]{:S(2)}) copy-start(bf16[512,256]{1,0:T(8,128)(2,1)} %constant.18.clone.x_hbm) | copy-start | bytes 786436
  7.3 0.9 %copy-start.6 = (bf16[512,128]{1,0:T(8,128)(2,1)S(1)}, bf16[512,128]{1,0:T(8,128)(2,1)}, u32[]{:S(2)}) copy-start(bf16[512,128]{1,0:T(8,128)(2,1)} %constant.20.clone.strip_hbm) | copy-start | bytes 393220
  8.2 0.9 %copy-start.7 = (bf16[3,1,16,1024]{3,2,1,0:T(8,128)(2,1)S(1)}, bf16[3,1,16,1024]{3,2,1,0:T(8,128)(2,1)}, u32[]{:S(2)}) copy-start(bf16[3,1,16,1024]{3,2,1,0:T(8,128)(2,1)} %velocity_hbm.1) | copy-start | bytes 294916
  9.1 0.9 %copy-start.8 = (bf16[96,512]{1,0:T(8,128)(2,1)S(1)}, bf16[96,512]{1,0:T(8,128)(2,1)}, u32[]{:S(2)}) copy-start(bf16[96,512]{1,0:T(8,128)(2,1)} %constant.17.clone.out_hbm) | copy-start | bytes 294916
  10.0 0.7 %copy-start.10 = (f32[512]{0:T(512)S(1)}, f32[512]{0:T(512)}, u32[]{:S(2)}) copy-start(f32[512]{0:T(512)} %constant.21.clone.profile) | copy-start | bytes 6148
  10.7 39.8 %copy-start.5 = (bf16[4,128,256]{2,1,0:T(8,128)(2,1)S(1)}, bf16[4,128,256]{2,1,0:T(8,128)(2,1)}, u32[]{:S(2)}) copy-start(bf16[4,128,256]{2,1,0:T(8,128)(2,1)} %constant.23.clone.ends) | copy-start | bytes 786436
  10.7 39.9 %copy-start.9 = (bf16[256,96]{1,0:T(8,128)(2,1)S(1)}, bf16[256,96]{1,0:T(8,128)(2,1)}, u32[]{:S(2)}) copy-start(bf16[256,96]{1,0:T(8,128)(2,1)} %constant.22.clone.spread) | copy-start | bytes 147460
  10.7 39.9 %copy-start.11 = (s32[2]{0:T(128)S(1)}, s32[2]{0:T(128)}, u32[]{:S(2)}) copy-start(s32[2]{0:T(128)} %shift.1) | copy-start | bytes 28

commit v2 on v1

--- a/solution.py
+++ b/solution.py
@@ -26,8 +26,10 @@
 CELLS = NZ * ROWS
 BLOCK = 256
 BLOCKS = NX // BLOCK
+PARTS = ((0, 3), (1, 2))
 ORDER = (0, 3, 1, 2)
 HALO = 3 * NZ
+WIDTH = 2 * BLOCK
 
 
 def band(coefs):
@@ -105,14 +107,14 @@
 
 
 def strip_in():
-    out = np.zeros((BLOCKS, 128, BLOCK))
+    out = np.zeros((2, 128, BLOCK))
     for lane in range(128):
         cell = lane % 4
         if cell < 3:
             if lane % 8 < 4:
                 out[0, lane, cell] = 1
             else:
-                out[BLOCKS - 1, lane, BLOCK - 3 + cell] = 1
+                out[1, lane, BLOCK - 3 + cell] = 1
     return out
 
 
@@ -135,8 +137,8 @@
 
 def exchange(
     tiles, profile, field_hbm, register_hbm, velocity_hbm, zy_hbm, out_hbm, x_hbm, edge_hbm, strip_hbm,
-    base, halo, strips,
-    field, register, vel, work, sums, zy, outw, xw, edgew, stripw,
+    base, field, halo, strips,
+    register, vel, work, sums, zy, outw, xw, edgew, stripw,
     load_sem, const_sem, vsend, vrecv, hsend, hrecv, ssend, srecv,
 ):
     t = lax.axis_index("tile")
@@ -146,35 +148,33 @@
     plus, minus = (xi + 1) % 4, (xi + 3) % 4
     opposite = (xi + 2) % 4
     other = hc + 2 - (hc // 2) * 4
-    at_plus, at_minus = plus * 4 + hc, minus * 4 + hc
+    at_plus, at_minus, at_opposite = plus * 4 + hc, minus * 4 + hc, opposite * 4 + hc
     partner = xi * 4 + other
     sibling = k + 1 - 2 * core
 
-    own_velocity = pltpu.make_async_copy(velocity_hbm.at[:, 0], vel.at[k], load_sem.at[0])
-    own_velocity.start()
-    load_field = pltpu.make_async_copy(field_hbm, field, load_sem.at[1])
-    load_field.start()
+    own_velocity = []
+    for i, (low, high, to) in enumerate(((0, 1, 0), (3, 4, 1), (1, 3, 2))):
+        source = velocity_hbm.at[:, 0, :, pl.ds(low * BLOCK, (high - low) * BLOCK)]
+        target = vel.at[k, :, :, pl.ds(to * BLOCK, (high - low) * BLOCK)]
+        own_velocity.append(pltpu.make_async_copy(source, target, load_sem.at[i]))
+    load_field = pltpu.make_async_copy(field_hbm, field, load_sem.at[3])
+    load_register = pltpu.make_async_copy(register_hbm, register, load_sem.at[4])
     pairs = ((zy_hbm, zy), (out_hbm, outw), (x_hbm, xw), (edge_hbm, edgew), (strip_hbm, stripw))
     consts = [pltpu.make_async_copy(a, b, const_sem.at[i]) for i, (a, b) in enumerate(pairs)]
-    for copy in consts:
+    for copy in (*own_velocity, load_field, *consts, load_register):
         copy.start()
-    load_register = pltpu.make_async_copy(register_hbm, register, load_sem.at[2])
-    load_register.start()
 
     barrier = pltpu.get_barrier_semaphore()
-    for peer in (at_plus, at_minus, partner, sibling):
+    for peer in (at_plus, at_minus, at_opposite, partner, sibling):
         pl.semaphore_signal(barrier, inc=1, device_id={"tf": peer})
     for step in range(1, tiles):
         pl.semaphore_signal(barrier, inc=1, device_id={"tile": (t + step) % tiles})
-    pl.semaphore_wait(barrier, 4 + tiles - 1)
+    pl.semaphore_wait(barrier, 5 + tiles - 1)
 
     started = []
 
-    def lanes(part):
-        return pl.ds(ORDER[part] * BLOCK, BLOCK)
-
     def plane_copy(plane, part, kind, peer):
-        block = vel.at[plane, :, :, lanes(part)]
+        block = vel.at[plane, :, :, pl.ds(part * WIDTH, WIDTH)]
         return pltpu.make_async_remote_copy(
             src_ref=block,
             dst_ref=block,
@@ -191,54 +191,43 @@
     def arrived(plane, part):
         plane_copy(plane, part, 0, sibling).wait_recv()
 
-    def of(x, h):
-        return x * 4 + h
-
-    own_velocity.wait()
-    for part in range(BLOCKS):
-        send(k, part, 0, partner)
-        send(k, part, 1, at_plus)
-        send(k, part, 2, at_minus)
-        send(k, part, 3, sibling)
-    for part in range(BLOCKS):
+    def send_own(part):
+        for kind, peer in enumerate((partner, at_opposite, at_plus, at_minus, sibling)):
+            send(k, part, kind, peer)
+
+    def relay(part):
         arrived(partner, part)
-        send(partner, part, 4, at_plus)
-        send(partner, part, 5, at_minus)
-        send(partner, part, 6, sibling)
-
-    def forward(part):
-        arrived(of(minus, hc), part)
-        send(of(minus, hc), part, 7, at_plus)
-        send(of(minus, hc), part, 8, sibling)
-        arrived(of(plus, hc), part)
-        send(of(plus, hc), part, 9, sibling)
-        arrived(of(plus, other), part)
-        send(of(plus, other), part, 10, at_minus)
-        send(of(plus, other), part, 11, sibling)
-        arrived(of(minus, other), part)
-        send(of(minus, other), part, 12, sibling)
-
-    def last_forward(part):
-        arrived(of(opposite, hc), part)
-        send(of(opposite, hc), part, 13, sibling)
-        arrived(of(opposite, other), part)
-        send(of(opposite, other), part, 14, sibling)
+        send(partner, part, 5, at_plus)
+        send(partner, part, 6, at_minus)
+        send(partner, part, 7, sibling)
+        arrived(at_opposite, part)
+        send(at_opposite, part, 8, partner)
+        send(at_opposite, part, 9, sibling)
+        arrived(at_plus, part)
+        send(at_plus, part, 10, sibling)
+        arrived(at_minus, part)
+        send(at_minus, part, 11, sibling)
+
+    def last_relay(part):
+        for i, x in enumerate((plus, minus, opposite)):
+            arrived(x * 4 + other, part)
+            send(x * 4 + other, part, 12 + i, sibling)
 
     def from_sibling(part):
-        flip = 1 - 2 * core
         for x in range(4):
             for h in range(2):
-                arrived(x * 4 + h * 2 + core + flip, part)
-
-    def emf_of(part):
-        block = lanes(part)
-        xpos = (lax.broadcasted_iota(jnp.int32, (ROWS, BLOCK), 1) + ORDER[part] * BLOCK).astype(F32)
+                arrived(x * 4 + h * 2 + 1 - core, part)
+
+    def emf_of(b):
+        block = pl.ds(b * BLOCK, BLOCK)
+        stored = pl.ds(ORDER.index(b) * BLOCK, BLOCK)
+        xpos = (lax.broadcasted_iota(jnp.int32, (ROWS, BLOCK), 1) + b * BLOCK).astype(F32)
         sweep = -SWEEP_SPEED * (2.0 * xpos / (NX - 1) - 1.0)
 
         def plane(z, carry):
             rows = pl.ds(pl.multiple_of(z * ROWS, ROWS), ROWS)
             f = [field[c, rows, block] for c in range(3)]
-            v = [vel[z, c, :, block].astype(F32) for c in range(3)]
+            v = [vel[z, c, :, stored].astype(F32) for c in range(3)]
             summed = [
                 (f[0] + profile[k * 32 + z]).astype(BF).astype(F32),
                 (f[1] + profile[k * 32 + 16 + z]).astype(BF).astype(F32),
@@ -257,28 +246,28 @@
 
         lax.fori_loop(0, NZ, plane, 0)
 
-    def halo_copies(part):
-        block = lanes(part)
+    def halo_copies(b):
+        block = pl.ds(b * BLOCK, BLOCK)
         out = []
         for side, peer in ((0, (t + 1) % tiles), (1, (t + tiles - 1) % tiles)):
             out.append(
                 pltpu.make_async_remote_copy(
                     src_ref=sums.at[:, side, :, block],
                     dst_ref=halo.at[:, side, :, block],
-                    send_sem=hsend.at[side, part],
-                    recv_sem=hrecv.at[side, part],
+                    send_sem=hsend.at[side, b],
+                    recv_sem=hrecv.at[side, b],
                     device_id={"tile": peer},
                 )
             )
         return out
 
-    def halo_of(part):
-        block = lanes(part)
+    def halo_of(b):
+        block = pl.ds(b * BLOCK, BLOCK)
         for c in range(3):
             total = dot(outw[...], work[c, CELLS:, block]).astype(BF)
             for side in range(2):
                 sums[c, side, :, block] = total[side * HALO : (side + 1) * HALO]
-        for copy in halo_copies(part):
+        for copy in halo_copies(b):
             copy.start()
             started.append(copy)
 
@@ -313,19 +302,24 @@
             copy.start()
             started.append(copy)
 
-    forward(0)
+    for copy in own_velocity:
+        copy.wait()
+    for part in range(2):
+        send_own(part)
+    for part in range(2):
+        relay(part)
     load_field.wait()
     for copy in consts:
         copy.wait()
-    for part in range(BLOCKS):
-        last_forward(part)
-        if part + 1 < BLOCKS:
-            forward(part + 1)
+    for part in range(2):
+        last_relay(part)
         from_sibling(part)
-        emf_of(part)
-        halo_of(part)
-        if part == 1:
+        for b in PARTS[part]:
+            emf_of(b)
+        if part == 0:
             strips_of()
+        for b in PARTS[part]:
+            halo_of(b)
 
     load_register.wait()
     for b in range(BLOCKS):
@@ -359,8 +353,8 @@
                 result -= TIME_STEP * STRETCH_RATE * field[0, :, block]
             base[c, :, block] = result
 
-    for part in range(BLOCKS):
-        for copy in halo_copies(part):
+    for b in range(BLOCKS):
+        for copy in halo_copies(b):
             copy.wait_recv()
     for step in range(1, tiles):
         strip_copy(step, (t + step) % tiles).wait_recv()
@@ -368,26 +362,36 @@
         copy.wait_send()
 
 
-def finish(shift, field, base, halo, strips, spread, ends, new_field, new_register, ghost):
-    @pl.when(pl.program_id(0) == 0)
-    def _():
-        t = lax.axis_index("tile")
-        total = strips.shape[1]
-        place = lax.broadcasted_iota(jnp.int32, (ROWS, total), 0) + t * ROWS
-        source = lax.broadcasted_iota(jnp.int32, (ROWS, total), 1)
-        lane = lax.broadcasted_iota(jnp.int32, (ROWS, 128), 1)
-        picks = [jnp.where((place + shift[side]) % total == source, 1.0, 0.0).astype(BF) for side in range(2)]
-        for c in range(3):
-            low, high = (dot(pick, strips[c]) for pick in picks)
-            both = jnp.where(lane % 8 < 4, low, high)
-            for z in range(NZ):
-                ghost[c, z * ROWS : (z + 1) * ROWS] = jnp.where(lane // 8 == z, both, 0.0).astype(BF)
-
+def finish(shift, base, field, halo, strips, spread, ends, field_out, register_out, ghost, new_field, new_register, sem):
+    t = lax.axis_index("tile")
+    total = strips.shape[1]
+    place = lax.broadcasted_iota(jnp.int32, (ROWS, total), 0) + t * ROWS
+    source = lax.broadcasted_iota(jnp.int32, (ROWS, total), 1)
+    lane = lax.broadcasted_iota(jnp.int32, (ROWS, 128), 1)
+    picks = [jnp.where((place + shift[side]) % total == source, 1.0, 0.0).astype(BF) for side in range(2)]
     for c in range(3):
-        total = dot(spread[...], halo[c].reshape(2 * HALO, BLOCK)) + dot(ghost[c], ends[0])
-        register = base[c] + SCALE * total
-        new_register[c] = register
-        new_field[c] = field[c] + RK_BETA * register
+        low, high = (dot(pick, strips[c]) for pick in picks)
+        both = jnp.where(lane % 8 < 4, low, high)
+        for z in range(NZ):
+            ghost[c, z * ROWS : (z + 1) * ROWS] = jnp.where(lane // 8 == z, both, 0.0).astype(BF)
+
+    copies = []
+    for c in range(3):
+        for b in range(BLOCKS):
+            block = slice(b * BLOCK, (b + 1) * BLOCK)
+            added = dot(spread[...], halo[c, :, :, block].reshape(2 * HALO, BLOCK))
+            if b in (0, BLOCKS - 1):
+                added += dot(ghost[c], ends[min(b, 1)])
+            register = base[c, :, block] + SCALE * added
+            new_register[c, :, block] = register
+            new_field[c, :, block] = field[c, :, block] + RK_BETA * register
+            for i, (here, there) in enumerate(((new_field, field_out), (new_register, register_out))):
+                where = (c, slice(None), pl.ds(b * BLOCK, BLOCK))
+                copy = pltpu.make_async_copy(here.at[where], there.at[where], sem.at[i, c, b])
+                copy.start()
+                copies.append(copy)
+    for copy in copies:
+        copy.wait()
 
 
 def body(tiles, test_field, register, velocity, shear_shift):
@@ -401,17 +405,17 @@
     anywhere = pl.BlockSpec(memory_space=pl.ANY)
     vmem = pl.BlockSpec(memory_space=pltpu.VMEM)
     dma = pltpu.SemaphoreType.DMA
-    base, halo, strips = pl.pallas_call(
+    base, kept, halo, strips = pl.pallas_call(
         functools.partial(exchange, tiles),
         out_shape=(
-            jax.ShapeDtypeStruct((3, CELLS, NX), F32),
-            jax.ShapeDtypeStruct((3, 2, HALO, NX), BF),
-            jax.ShapeDtypeStruct((3, tiles * ROWS, 128), BF),
+            pltpu.VMEM((3, CELLS, NX), F32),
+            pltpu.VMEM((3, CELLS, NX), F32),
+            pltpu.VMEM((3, 2, HALO, NX), BF),
+            pltpu.VMEM((3, tiles * ROWS, 128), BF),
         ),
         in_specs=[pl.BlockSpec(memory_space=pltpu.SMEM)] + [anywhere] * 8,
-        out_specs=(vmem, vmem, vmem),
+        out_specs=(vmem,) * 4,
         scratch_shapes=[
-            pltpu.VMEM((3, CELLS, NX), F32),
             pltpu.VMEM((3, CELLS, NX), F32),
             pltpu.VMEM((16, 3, ROWS, NX), BF),
             pltpu.VMEM((3, 3 * CELLS, NX), BF),
@@ -421,41 +425,36 @@
             pltpu.VMEM(xw.shape, BF),
             pltpu.VMEM(edgew.shape, BF),
             pltpu.VMEM(stripw.shape, BF),
-            dma((3,)),
             dma((5,)),
-            dma((BLOCKS, 15)),
-            dma((BLOCKS, 16)),
+            dma((5,)),
+            dma((2, 15)),
+            dma((2, 16)),
             dma((2, BLOCKS)),
             dma((2, BLOCKS)),
             dma((tiles,)),
             dma((tiles,)),
         ],
         compiler_params=pltpu.CompilerParams(
-            collective_id=0, has_side_effects=True, vmem_limit_bytes=40 * 2**20
+            collective_id=0, has_side_effects=True, vmem_limit_bytes=54 * 2**20
         ),
         name="exchange",
     )(jnp.asarray(profiles()), field, reg, velocity, zy, outw, xw, edgew, stripw)
 
     spread, ends = small(halo_in()), small(strip_in())
-    whole = pl.BlockSpec((3, CELLS, BLOCK), lambda b: (0, 0, b))
     new_field, new_register = pl.pallas_call(
         finish,
-        grid=(BLOCKS,),
         out_shape=(jax.ShapeDtypeStruct((3, CELLS, NX), F32),) * 2,
-        in_specs=[
-            pl.BlockSpec(memory_space=pltpu.SMEM),
-            whole,
-            whole,
-            pl.BlockSpec((3, 2, HALO, BLOCK), lambda b: (0, 0, 0, b)),
-            pl.BlockSpec((3, tiles * ROWS, 128), lambda b: (0, 0, 0)),
-            pl.BlockSpec((CELLS, 2 * HALO), lambda b: (0, 0)),
-            pl.BlockSpec((1, 128, BLOCK), lambda b: (b, 0, 0)),
+        in_specs=[pl.BlockSpec(memory_space=pltpu.SMEM)] + [vmem] * 6,
+        out_specs=(anywhere, anywhere),
+        scratch_shapes=[
+            pltpu.VMEM((3, CELLS, 128), BF),
+            pltpu.VMEM((3, CELLS, NX), F32),
+            pltpu.VMEM((3, CELLS, NX), F32),
+            dma((2, 3, BLOCKS)),
         ],
-        out_specs=(whole, whole),
-        scratch_shapes=[pltpu.VMEM((3, CELLS, 128), BF)],
         compiler_params=pltpu.CompilerParams(vmem_limit_bytes=24 * 2**20),
         name="finish",
-    )(shear_shift, field, base, halo, strips, spread, ends)
+    )(shear_shift, base, kept, halo, strips, spread, ends)
     return new_field.reshape(test_field.shape), new_register.reshape(register.shape)
 
 

time: 55.5 us -> 40.7 us (0.73)
  local copies, waits for them, and re-layouts: 10 us -> 0.02 us
  Pallas kernels: 44.4 us -> 39.9 us
    unnamed x24 -> x6, local copies, waits for them, and re-layouts: 10 us -> 0.02 us
    pallas_call x2, Pallas kernels: 44.4 us -> 39.9 us  [the longest x1 36.1 us: body(): pl.pallas_call(functools.partial(exchange, tiles), out_shape=(pltpu.VMEM(...]
where the time goes in v2:
time: 40.7 us; the launch traced here: 40.6 us
  Pallas kernels  39.9 us (98%)
  between operations  0.69 us (2%)
    pallas_call x1, Pallas kernels, body(): pl.pallas_call(functools.partial(exchange, tiles), out_shape=(pltpu.VMEM(...  36.1 us
    pallas_call x1, Pallas kernels, body(): pl.pallas_call(finish, out_shape=(jax.ShapeDtypeStruct((3, CELLS, NX), F3...  3.81 us

profile of v2, /device:TPU:1, one launch (start us, length us, event | category | flops | bytes accessed | tf_op | source)
XLA Modules:
  0.0 40.6 jit_solution(10374149946521419257)
XLA Ops:
  0.6 0.0 copy-start
  0.6 0.0 copy-start.1
  0.7 0.0 copy-start.2
  0.7 36.1 %exchange.1 = (f32[3,256,1024]{2,1,0:T(8,128)S(1)}, f32[3,256,1024]{2,1,0:T(8,128)S(1)}, bf16[3,2,48,1024]{3,2,1,0:T(8,128)(2,1)S(1)}, bf16[3,256,128]{2,1,0:T(8,128)(2,1)S(1)}) custom-call(f32[512]{0:T(512)} %constant.21.clone.profile, f32[3,256,1024]{2,1,0:T(8,128)} %bitcast.4, f32[3,256,1024]{2,1,0:T(8,128)} %bitcast.5, ...), custom_call_target="tpu_custom_call" | custom-call | tf_op jit(solution)/shard_map/exchange/pallas_call | solution.py:408
  36.7 0.0 copy-done
  36.7 0.0 copy-done.1
  36.8 0.0 copy-done.2
  36.8 3.8 %finish.1 = (f32[3,256,1024]{2,1,0:T(8,128)}, f32[3,256,1024]{2,1,0:T(8,128)}) custom-call(s32[2]{0:T(128)S(1)} %copy-done.2, f32[3,256,1024]{2,1,0:T(8,128)S(1)} %get-tuple-element.8.base, f32[3,256,1024]{2,1,0:T(8,128)S(1)} %get-tuple-element.9.field, bf16[3,2,48,1024]{3,2,1,0:T(8,128)(2,1)S(1)} %get-tuple-element.10.halo, ...), custom_call_target="tpu_custom_call" | custom-call | tf_op jit(solution)/shard_map/finish/pallas_call | solution.py:444
Async XLA Ops:
  0.6 36.1 %copy-start = (bf16[2,128,256]{2,1,0:T(8,128)(2,1)S(1)}, bf16[2,128,256]{2,1,0:T(8,128)(2,1)}, u32[]{:S(2)}) copy-start(bf16[2,128,256]{2,1,0:T(8,128)(2,1)} %constant.23.clone.ends) | copy-start | bytes 393220
  0.6 36.1 %copy-start.1 = (bf16[256,96]{1,0:T(8,128)(2,1)S(1)}, bf16[256,96]{1,0:T(8,128)(2,1)}, u32[]{:S(2)}) copy-start(bf16[256,96]{1,0:T(8,128)(2,1)} %constant.22.clone.spread) | copy-start | bytes 147460
  0.7 36.1 %copy-start.2 = (s32[2]{0:T(128)S(1)}, s32[2]{0:T(128)}, u32[]{:S(2)}) copy-start(s32[2]{0:T(128)} %shift.1) | copy-start | bytes 28

commit v3 on v2

--- a/solution.py
+++ b/solution.py
@@ -26,10 +26,12 @@
 CELLS = NZ * ROWS
 BLOCK = 256
 BLOCKS = NX // BLOCK
-PARTS = ((0, 3), (1, 2))
+PARTS = ((0, 3), (1,), (2,))
+SPANS = ((0, 2), (2, 1), (3, 1))
 ORDER = (0, 3, 1, 2)
 HALO = 3 * NZ
-WIDTH = 2 * BLOCK
+NEAR = (-2, -1, 1, 2)
+FAR = (1, 2, 3)
 
 
 def band(coefs):
@@ -136,10 +138,10 @@
 
 
 def exchange(
-    tiles, profile, field_hbm, register_hbm, velocity_hbm, zy_hbm, out_hbm, x_hbm, edge_hbm, strip_hbm,
-    base, field, halo, strips,
-    register, vel, work, sums, zy, outw, xw, edgew, stripw,
-    load_sem, const_sem, vsend, vrecv, hsend, hrecv, ssend, srecv,
+    tiles, shift, profile, field_hbm, register_hbm, velocity_hbm, zy_hbm, out_hbm, x_hbm, edge_hbm, strip_hbm,
+    base, field, halo, wide,
+    register, vel, work, sums, zy, outw, xw, edgew, stripw, near,
+    load_sem, const_sem, vsend, vrecv, hsend, hrecv, nsend, nrecv, wsend, wrecv, told,
 ):
     t = lax.axis_index("tile")
     k = lax.axis_index("tf")
@@ -167,14 +169,24 @@
     barrier = pltpu.get_barrier_semaphore()
     for peer in (at_plus, at_minus, at_opposite, partner, sibling):
         pl.semaphore_signal(barrier, inc=1, device_id={"tf": peer})
-    for step in range(1, tiles):
+    for step in (1, tiles // 2, tiles - 1):
         pl.semaphore_signal(barrier, inc=1, device_id={"tile": (t + step) % tiles})
-    pl.semaphore_wait(barrier, 5 + tiles - 1)
+    pl.semaphore_wait(barrier, 5 + 3)
+
+    def tell(round_, step):
+        for side, to in enumerate((step, tiles - step)):
+            pl.semaphore_signal(told.at[round_, side], inc=1, device_id={"tile": (t + to) % tiles})
+
+    def hear(round_):
+        for side in range(2):
+            pl.semaphore_wait(told.at[round_, side], 1)
+
+    tell(0, 1)
 
     started = []
 
     def plane_copy(plane, part, kind, peer):
-        block = vel.at[plane, :, :, pl.ds(part * WIDTH, WIDTH)]
+        block = vel.at[plane, :, :, pl.ds(SPANS[part][0] * BLOCK, SPANS[part][1] * BLOCK)]
         return pltpu.make_async_remote_copy(
             src_ref=block,
             dst_ref=block,
@@ -271,13 +283,23 @@
             copy.start()
             started.append(copy)
 
-    def strip_copy(step, at):
+    def near_copy(i):
+        slot = 2 - NEAR[i]
         return pltpu.make_async_remote_copy(
-            src_ref=strips.at[:, pl.ds(pl.multiple_of(at * ROWS, ROWS), ROWS), :],
-            dst_ref=strips.at[:, pl.ds(pl.multiple_of(at * ROWS, ROWS), ROWS), :],
-            send_sem=ssend.at[step],
-            recv_sem=srecv.at[at],
-            device_id={"tile": (t + step) % tiles},
+            src_ref=near.at[:, 2],
+            dst_ref=near.at[:, slot],
+            send_sem=nsend.at[i],
+            recv_sem=nrecv.at[slot],
+            device_id={"tile": (t + NEAR[i] + tiles) % tiles},
+        )
+
+    def wide_copy(i):
+        return pltpu.make_async_remote_copy(
+            src_ref=wide.at[:, 0],
+            dst_ref=wide.at[:, FAR[i]],
+            send_sem=wsend.at[i],
+            recv_sem=wrecv.at[i],
+            device_id={"tile": (t + tiles - 4 * FAR[i]) % tiles},
         )
 
     def strips_of():
@@ -296,22 +318,42 @@
             if c == 2:
                 total += dot(ends(0, 0), stripw[256:])
             packed = jnp.sum(jnp.where(own, total, 0.0).reshape(NZ, ROWS, 128), axis=0)
-            strips[c, pl.ds(pl.multiple_of(t * ROWS, ROWS), ROWS), :] = packed.astype(BF)
-        for step in range(1, tiles):
-            copy = strip_copy(step, t)
+            near[c, 2] = packed.astype(BF)
+        for i in range(4):
+            copy = near_copy(i)
             copy.start()
             started.append(copy)
 
+    def shifted_strips():
+        for i in range(4):
+            near_copy(i).wait_recv()
+        row = lax.broadcasted_iota(jnp.int32, (ROWS, 5 * ROWS), 0)
+        source = lax.broadcasted_iota(jnp.int32, (ROWS, 5 * ROWS), 1)
+        lane = lax.broadcasted_iota(jnp.int32, (ROWS, 128), 1)
+        picks = [
+            jnp.where(row + ((shift[side] + 2 * ROWS) & (4 * ROWS - 1)) == source, 1.0, 0.0).astype(BF) for side in range(2)
+        ]
+        for c in range(3):
+            low, high = (dot(pick, near[c].reshape(5 * ROWS, 128)) for pick in picks)
+            wide[c, 0] = jnp.where(lane % 8 < 4, low, high).astype(BF)
+        hear(1)
+        for i in range(3):
+            copy = wide_copy(i)
+            copy.start()
+            started.append(copy)
+
     for copy in own_velocity:
         copy.wait()
-    for part in range(2):
+    for part in range(3):
         send_own(part)
-    for part in range(2):
+    for part in range(3):
         relay(part)
+    hear(0)
+    tell(1, 2)
     load_field.wait()
     for copy in consts:
         copy.wait()
-    for part in range(2):
+    for part in range(3):
         last_relay(part)
         from_sibling(part)
         for b in PARTS[part]:
@@ -320,6 +362,7 @@
             strips_of()
         for b in PARTS[part]:
             halo_of(b)
+    shifted_strips()
 
     load_register.wait()
     for b in range(BLOCKS):
@@ -356,22 +399,17 @@
     for b in range(BLOCKS):
         for copy in halo_copies(b):
             copy.wait_recv()
-    for step in range(1, tiles):
-        strip_copy(step, (t + step) % tiles).wait_recv()
+    for i in range(3):
+        wide_copy(i).wait_recv()
     for copy in started:
         copy.wait_send()
 
 
 def finish(shift, base, field, halo, strips, spread, ends, field_out, register_out, ghost, new_field, new_register, sem):
-    t = lax.axis_index("tile")
-    total = strips.shape[1]
-    place = lax.broadcasted_iota(jnp.int32, (ROWS, total), 0) + t * ROWS
-    source = lax.broadcasted_iota(jnp.int32, (ROWS, total), 1)
     lane = lax.broadcasted_iota(jnp.int32, (ROWS, 128), 1)
-    picks = [jnp.where((place + shift[side]) % total == source, 1.0, 0.0).astype(BF) for side in range(2)]
+    steps = [((shift[side] + 2 * ROWS) // (4 * ROWS)) % 4 for side in range(2)]
     for c in range(3):
-        low, high = (dot(pick, strips[c]) for pick in picks)
-        both = jnp.where(lane % 8 < 4, low, high)
+        both = jnp.where(lane % 8 < 4, strips[c, steps[0]], strips[c, steps[1]]).astype(F32)
         for z in range(NZ):
             ghost[c, z * ROWS : (z + 1) * ROWS] = jnp.where(lane // 8 == z, both, 0.0).astype(BF)
 
@@ -405,15 +443,15 @@
     anywhere = pl.BlockSpec(memory_space=pl.ANY)
     vmem = pl.BlockSpec(memory_space=pltpu.VMEM)
     dma = pltpu.SemaphoreType.DMA
-    base, kept, halo, strips = pl.pallas_call(
+    base, kept, halo, wide = pl.pallas_call(
         functools.partial(exchange, tiles),
         out_shape=(
             pltpu.VMEM((3, CELLS, NX), F32),
             pltpu.VMEM((3, CELLS, NX), F32),
             pltpu.VMEM((3, 2, HALO, NX), BF),
-            pltpu.VMEM((3, tiles * ROWS, 128), BF),
+            pltpu.VMEM((3, 4, ROWS, 128), BF),
         ),
-        in_specs=[pl.BlockSpec(memory_space=pltpu.SMEM)] + [anywhere] * 8,
+        in_specs=[pl.BlockSpec(memory_space=pltpu.SMEM)] * 2 + [anywhere] * 8,
         out_specs=(vmem,) * 4,
         scratch_shapes=[
             pltpu.VMEM((3, CELLS, NX), F32),
@@ -425,20 +463,24 @@
             pltpu.VMEM(xw.shape, BF),
             pltpu.VMEM(edgew.shape, BF),
             pltpu.VMEM(stripw.shape, BF),
+            pltpu.VMEM((3, 5, ROWS, 128), BF),
             dma((5,)),
             dma((5,)),
-            dma((2, 15)),
-            dma((2, 16)),
+            dma((3, 15)),
+            dma((3, 16)),
             dma((2, BLOCKS)),
             dma((2, BLOCKS)),
-            dma((tiles,)),
-            dma((tiles,)),
+            dma((4,)),
+            dma((5,)),
+            dma((3,)),
+            dma((3,)),
+            pltpu.SemaphoreType.REGULAR((2, 2)),
         ],
         compiler_params=pltpu.CompilerParams(
             collective_id=0, has_side_effects=True, vmem_limit_bytes=54 * 2**20
         ),
         name="exchange",
-    )(jnp.asarray(profiles()), field, reg, velocity, zy, outw, xw, edgew, stripw)
+    )(shear_shift, jnp.asarray(profiles()), field, reg, velocity, zy, outw, xw, edgew, stripw)
 
     spread, ends = small(halo_in()), small(strip_in())
     new_field, new_register = pl.pallas_call(
@@ -454,7 +496,7 @@
         ],
         compiler_params=pltpu.CompilerParams(vmem_limit_bytes=24 * 2**20),
         name="finish",
-    )(shear_shift, base, kept, halo, strips, spread, ends)
+    )(shear_shift, base, kept, halo, wide, spread, ends)
     return new_field.reshape(test_field.shape), new_register.reshape(register.shape)
 
 

time: 40.7 us -> 38 us (0.934)
  Pallas kernels: 39.9 us -> 37.2 us
    pallas_call x1, Pallas kernels: 36.1 us -> 33.5 us  [body(): pl.pallas_call(functools.partial(exchange, tiles), out_shape=(pltpu.VMEM(...]
where the time goes in v3:
time: 38 us; the launch traced here: 37.9 us
  Pallas kernels  37.2 us (98%)
  between operations  0.69 us (2%)
    pallas_call x1, Pallas kernels, body(): pl.pallas_call(functools.partial(exchange, tiles), out_shape=(pltpu.VMEM(...  33.5 us
    pallas_call x1, Pallas kernels, body(): pl.pallas_call(finish, out_shape=(jax.ShapeDtypeStruct((3, CELLS, NX), F3...  3.7 us

profile of v3, /device:TPU:1, one launch (start us, length us, event | category | flops | bytes accessed | tf_op | source)
XLA Modules:
  0.0 37.9 jit_solution(11317135271619370162)
XLA Ops:
  0.6 0.0 copy-start
  0.6 0.0 copy-start.1
  0.7 0.0 copy-start.2
  0.7 33.5 %exchange.1 = (f32[3,256,1024]{2,1,0:T(8,128)S(1)}, f32[3,256,1024]{2,1,0:T(8,128)S(1)}, bf16[3,2,48,1024]{3,2,1,0:T(8,128)(2,1)S(1)}, bf16[3,4,16,128]{3,2,1,0:T(8,128)(2,1)S(1)}) custom-call(s32[2]{0:T(128)} %shift.3, f32[512]{0:T(512)} %constant.21.clone.profile, f32[3,256,1024]{2,1,0:T(8,128)} %bitcast.4, f32[3,256,1024]{2,1,0:T(8,128)} %bitcast.5, ...), custom_call_target="tpu_custom_call" | custom-call | tf_op jit(solution)/shard_map/exchange/pallas_call | solution.py:446
  34.2 0.0 copy-done
  34.2 0.0 copy-done.1
  34.2 0.0 copy-done.2
  34.2 3.7 %finish.1 = (f32[3,256,1024]{2,1,0:T(8,128)}, f32[3,256,1024]{2,1,0:T(8,128)}) custom-call(s32[2]{0:T(128)S(1)} %copy-done.2, f32[3,256,1024]{2,1,0:T(8,128)S(1)} %get-tuple-element.8.base, f32[3,256,1024]{2,1,0:T(8,128)S(1)} %get-tuple-element.9.field, bf16[3,2,48,1024]{3,2,1,0:T(8,128)(2,1)S(1)} %get-tuple-element.10.halo, ...), custom_call_target="tpu_custom_call" | custom-call | tf_op jit(solution)/shard_map/finish/pallas_call | solution.py:486
Async XLA Ops:
  0.6 33.5 %copy-start = (bf16[2,128,256]{2,1,0:T(8,128)(2,1)S(1)}, bf16[2,128,256]{2,1,0:T(8,128)(2,1)}, u32[]{:S(2)}) copy-start(bf16[2,128,256]{2,1,0:T(8,128)(2,1)} %constant.23.clone.ends) | copy-start | bytes 393220
  0.6 33.5 %copy-start.1 = (bf16[256,96]{1,0:T(8,128)(2,1)S(1)}, bf16[256,96]{1,0:T(8,128)(2,1)}, u32[]{:S(2)}) copy-start(bf16[256,96]{1,0:T(8,128)(2,1)} %constant.22.clone.spread) | copy-start | bytes 147460
  0.7 33.5 %copy-start.2 = (s32[2]{0:T(128)S(1)}, s32[2]{0:T(128)}, u32[]{:S(2)}) copy-start(s32[2]{0:T(128)} %shift.3) | copy-start | bytes 28

commit v4 on v3

--- a/solution.py
+++ b/solution.py
@@ -32,6 +32,7 @@
 HALO = 3 * NZ
 NEAR = (-2, -1, 1, 2)
 FAR = (1, 2, 3)
+SENT = (0, 2, 1)
 
 
 def band(coefs):
@@ -138,9 +139,9 @@
 
 
 def exchange(
-    tiles, shift, profile, field_hbm, register_hbm, velocity_hbm, zy_hbm, out_hbm, x_hbm, edge_hbm, strip_hbm,
+    tiles, shift, profile, field_hbm, register_hbm, velocity_hbm, own_hbm, zy_hbm, out_hbm, x_hbm, edge_hbm, strip_hbm,
     base, field, halo, wide,
-    register, vel, work, sums, zy, outw, xw, edgew, stripw, near,
+    register, vel, work, emf, sums, waiting, kept_strips, ownw, zy, outw, xw, edgew, stripw, near,
     load_sem, const_sem, vsend, vrecv, hsend, hrecv, nsend, nrecv, wsend, wrecv, told,
 ):
     t = lax.axis_index("tile")
@@ -161,7 +162,7 @@
         own_velocity.append(pltpu.make_async_copy(source, target, load_sem.at[i]))
     load_field = pltpu.make_async_copy(field_hbm, field, load_sem.at[3])
     load_register = pltpu.make_async_copy(register_hbm, register, load_sem.at[4])
-    pairs = ((zy_hbm, zy), (out_hbm, outw), (x_hbm, xw), (edge_hbm, edgew), (strip_hbm, stripw))
+    pairs = ((own_hbm, ownw), (zy_hbm, zy), (out_hbm, outw), (x_hbm, xw), (edge_hbm, edgew), (strip_hbm, stripw))
     consts = [pltpu.make_async_copy(a, b, const_sem.at[i]) for i, (a, b) in enumerate(pairs)]
     for copy in (*own_velocity, load_field, *consts, load_register):
         copy.start()
@@ -230,55 +231,104 @@
             for h in range(2):
                 arrived(x * 4 + h * 2 + 1 - core, part)
 
+    def prepare(b):
+        block = pl.ds(b * BLOCK, BLOCK)
+        xpos = (lax.broadcasted_iota(jnp.int32, (ROWS, BLOCK), 1) + b * BLOCK).astype(F32)
+        sweep = -SWEEP_SPEED * (2.0 * xpos / (NX - 1) - 1.0)
+
+        def plane(z, carry):
+            rows = pl.ds(pl.multiple_of(z * ROWS, ROWS), ROWS)
+            below = pl.ds(pl.multiple_of(CELLS + z * ROWS, ROWS), ROWS)
+            for c in range(3):
+                f = field[c, rows, block]
+                work[c, rows, block] = (-(sweep * f)).astype(BF)
+                work[c, below, block] = (f * (1.0 / 30.0)).astype(BF)
+            return carry
+
+        lax.fori_loop(0, NZ, plane, 0)
+
     def emf_of(b):
         block = pl.ds(b * BLOCK, BLOCK)
         stored = pl.ds(ORDER.index(b) * BLOCK, BLOCK)
-        xpos = (lax.broadcasted_iota(jnp.int32, (ROWS, BLOCK), 1) + b * BLOCK).astype(F32)
-        sweep = -SWEEP_SPEED * (2.0 * xpos / (NX - 1) - 1.0)
 
         def plane(z, carry):
             rows = pl.ds(pl.multiple_of(z * ROWS, ROWS), ROWS)
-            f = [field[c, rows, block] for c in range(3)]
             v = [vel[z, c, :, stored].astype(F32) for c in range(3)]
             summed = [
-                (f[0] + profile[k * 32 + z]).astype(BF).astype(F32),
-                (f[1] + profile[k * 32 + 16 + z]).astype(BF).astype(F32),
-                f[2].astype(BF).astype(F32),
+                (field[0, rows, block] + profile[k * 32 + z]).astype(BF).astype(F32),
+                (field[1, rows, block] + profile[k * 32 + 16 + z]).astype(BF).astype(F32),
+                field[2, rows, block].astype(BF).astype(F32),
             ]
             emf_x = v[1] * summed[2] - v[2] * summed[1]
             emf_y = v[2] * summed[0] - v[0] * summed[2]
             emf_z = v[0] * summed[1] - v[1] * summed[0]
-            mixed = (emf_z - sweep * f[0], -(sweep * f[1]), -emf_x - sweep * f[2])
-            for c, value in enumerate((-emf_y, emf_x, emf_z)):
-                work[c, rows, block] = value.astype(BF)
-            for c in range(3):
-                work[c, pl.ds(pl.multiple_of(CELLS + z * ROWS, ROWS), ROWS), block] = mixed[c].astype(BF)
-                work[c, pl.ds(pl.multiple_of(2 * CELLS + z * ROWS, ROWS), ROWS), block] = (f[c] * (1.0 / 30.0)).astype(BF)
+            for i, value in enumerate((-emf_y, emf_z, -emf_x)):
+                emf[pl.ds(pl.multiple_of(i * CELLS + z * ROWS, ROWS), ROWS), block] = value.astype(BF)
             return carry
 
         lax.fori_loop(0, NZ, plane, 0)
 
+    def sides(array, b):
+        before = array[:, b * BLOCK - 128 : b * BLOCK] if b > 0 else None
+        after = array[:, (b + 1) * BLOCK : (b + 1) * BLOCK + 128] if b + 1 < BLOCKS else None
+        if before is None:
+            return after, slice(128, 256)
+        if after is None:
+            return before, slice(0, 128)
+        return jnp.concatenate([before, after], axis=1), slice(0, 256)
+
+    def along_x(array, b, weights):
+        far, rows = sides(array, b)
+        return dot(array[:, b * BLOCK : (b + 1) * BLOCK], xw[weights]) + dot(far, edgew[weights][rows])
+
+    def field_part(b):
+        block = slice(b * BLOCK, (b + 1) * BLOCK)
+        for place, c in enumerate(SENT):
+            total = dot(outw[...], work[c, :, block])
+            if place < 2:
+                waiting[place, :, block] = total
+            else:
+                for side in range(2):
+                    sums[2, side, :, block] = total[side * HALO : (side + 1) * HALO].astype(BF)
+        for c in range(3):
+            total = dot(ownw[...], work[c, :, block]) + along_x(work.at[c, CELLS:], b, slice(0, 256))
+            result = RK_ALPHA * register[c, :, block] + SCALE * total
+            if c == 1:
+                result -= TIME_STEP * STRETCH_RATE * field[0, :, block]
+            base[c, :, block] = result
+
+    def emf_part_zy(b):
+        block = slice(b * BLOCK, (b + 1) * BLOCK)
+        base[0, :, block] += SCALE * dot(zy[...], emf[: 2 * CELLS, block])
+        base[1, :, block] -= SCALE * dot(zy[:, :CELLS], emf[2 * CELLS :, block])
+        base[2, :, block] += SCALE * dot(zy[:, CELLS:], emf[2 * CELLS :, block])
+
+    def emf_part_x(b):
+        block = slice(b * BLOCK, (b + 1) * BLOCK)
+        base[1, :, block] += SCALE * along_x(emf.at[CELLS : 2 * CELLS], b, slice(256, 512))
+        base[2, :, block] += SCALE * along_x(emf.at[:CELLS], b, slice(256, 512))
+
+    def halo_copy(side, places, block, i):
+        return pltpu.make_async_remote_copy(
+            src_ref=sums.at[places, side, :, block],
+            dst_ref=halo.at[places, side, :, block],
+            send_sem=hsend.at[side, i],
+            recv_sem=hrecv.at[side, i],
+            device_id={"tile": (t + (1, tiles - 1)[side]) % tiles},
+        )
+
     def halo_copies(b):
-        block = pl.ds(b * BLOCK, BLOCK)
-        out = []
-        for side, peer in ((0, (t + 1) % tiles), (1, (t + tiles - 1) % tiles)):
-            out.append(
-                pltpu.make_async_remote_copy(
-                    src_ref=sums.at[:, side, :, block],
-                    dst_ref=halo.at[:, side, :, block],
-                    send_sem=hsend.at[side, b],
-                    recv_sem=hrecv.at[side, b],
-                    device_id={"tile": peer},
-                )
-            )
-        return out
+        return [halo_copy(side, pl.ds(0, 2), pl.ds(b * BLOCK, BLOCK), b) for side in range(2)]
+
+    def y_halo_copies():
+        return [halo_copy(side, pl.ds(2, 1), pl.ds(0, NX), BLOCKS) for side in range(2)]
 
     def halo_of(b):
-        block = pl.ds(b * BLOCK, BLOCK)
-        for c in range(3):
-            total = dot(outw[...], work[c, CELLS:, block]).astype(BF)
+        block = slice(b * BLOCK, (b + 1) * BLOCK)
+        for place, first in enumerate((CELLS, 2 * CELLS)):
+            total = waiting[place, :, block] + dot(outw[:, :CELLS], emf[first : first + CELLS, block])
             for side in range(2):
-                sums[c, side, :, block] = total[side * HALO : (side + 1) * HALO]
+                sums[place, side, :, block] = total[side * HALO : (side + 1) * HALO].astype(BF)
         for copy in halo_copies(b):
             copy.start()
             started.append(copy)
@@ -302,23 +352,21 @@
             device_id={"tile": (t + tiles - 4 * FAR[i]) % tiles},
         )
 
-    def strips_of():
+    def strip_sum(array, weights):
         row = lax.broadcasted_iota(jnp.int32, (CELLS, 128), 0)
         lane = lax.broadcasted_iota(jnp.int32, (CELLS, 128), 1)
-        own = (row // ROWS) == (lane // 8)
-
-        def ends(c, part):
-            rows = slice(part * CELLS, (part + 1) * CELLS)
-            return jnp.concatenate([work[c, rows, :128], work[c, rows, NX - 128 :]], axis=1)
-
+        ends = jnp.concatenate([array[:, :128], array[:, NX - 128 :]], axis=1)
+        own = jnp.where((row // ROWS) == (lane // 8), dot(ends, stripw[weights]), 0.0)
+        return jnp.sum(own.reshape(NZ, ROWS, 128), axis=0)
+
+    def field_strips():
         for c in range(3):
-            total = dot(ends(c, 2), stripw[:256])
-            if c == 1:
-                total += dot(ends(2, 0), stripw[256:])
-            if c == 2:
-                total += dot(ends(0, 0), stripw[256:])
-            packed = jnp.sum(jnp.where(own, total, 0.0).reshape(NZ, ROWS, 128), axis=0)
-            near[c, 2] = packed.astype(BF)
+            kept_strips[c] = strip_sum(work.at[c, CELLS:], slice(0, 256))
+
+    def strips_of():
+        near[0, 2] = kept_strips[0].astype(BF)
+        near[1, 2] = (kept_strips[1] + strip_sum(emf.at[CELLS : 2 * CELLS], slice(256, 512))).astype(BF)
+        near[2, 2] = (kept_strips[2] + strip_sum(emf.at[:CELLS], slice(256, 512))).astype(BF)
         for i in range(4):
             copy = near_copy(i)
             copy.start()
@@ -346,14 +394,27 @@
         copy.wait()
     for part in range(3):
         send_own(part)
-    for part in range(3):
-        relay(part)
+    load_field.wait()
+    for b in range(BLOCKS):
+        prepare(b)
+    for copy in consts:
+        copy.wait()
+    load_register.wait()
+    field_part(0)
+    field_part(3)
+    relay(0)
+    field_strips()
+    field_part(1)
+    relay(1)
+    field_part(2)
+    for copy in y_halo_copies():
+        copy.start()
+        started.append(copy)
+    relay(2)
     hear(0)
     tell(1, 2)
-    load_field.wait()
-    for copy in consts:
-        copy.wait()
-    for part in range(3):
+
+    def finish_part(part):
         last_relay(part)
         from_sibling(part)
         for b in PARTS[part]:
@@ -362,40 +423,20 @@
             strips_of()
         for b in PARTS[part]:
             halo_of(b)
+
+    finish_part(0)
+    emf_part_zy(0)
+    finish_part(1)
+    emf_part_zy(3)
+    emf_part_x(0)
     shifted_strips()
-
-    load_register.wait()
-    for b in range(BLOCKS):
-        block = slice(b * BLOCK, (b + 1) * BLOCK)
-
-        def ends(c, part):
-            rows = slice(part * CELLS, (part + 1) * CELLS)
-            before = work[c, rows, b * BLOCK - 128 : b * BLOCK] if b > 0 else None
-            after = work[c, rows, (b + 1) * BLOCK : (b + 1) * BLOCK + 128] if b + 1 < BLOCKS else None
-            if before is None:
-                return after, slice(128, 256)
-            if after is None:
-                return before, slice(0, 128)
-            return jnp.concatenate([before, after], axis=1), slice(0, 256)
-
-        for c in range(3):
-            if c < 2:
-                total = dot(zy[...], work[c, :, block])
-            else:
-                total = dot(zy[:, CELLS:], work[c, CELLS:, block])
-            total += dot(work[c, 2 * CELLS :, block], xw[:256])
-            far, near = ends(c, 2)
-            total += dot(far, edgew[:256][near])
-            if c > 0:
-                source = 2 if c == 1 else 0
-                total += dot(work[source, :CELLS, block], xw[256:])
-                far, near = ends(source, 0)
-                total += dot(far, edgew[256:][near])
-            result = RK_ALPHA * register[c, :, block] + SCALE * total
-            if c == 1:
-                result -= TIME_STEP * STRETCH_RATE * field[0, :, block]
-            base[c, :, block] = result
-
+    finish_part(2)
+    emf_part_zy(1)
+    emf_part_zy(2)
+    for b in (1, 2, 3):
+        emf_part_x(b)
+    for copy in y_halo_copies():
+        copy.wait_recv()
     for b in range(BLOCKS):
         for copy in halo_copies(b):
             copy.wait_recv()
@@ -417,7 +458,7 @@
     for c in range(3):
         for b in range(BLOCKS):
             block = slice(b * BLOCK, (b + 1) * BLOCK)
-            added = dot(spread[...], halo[c, :, :, block].reshape(2 * HALO, BLOCK))
+            added = dot(spread[...], halo[SENT.index(c), :, :, block].reshape(2 * HALO, BLOCK))
             if b in (0, BLOCKS - 1):
                 added += dot(ghost[c], ends[min(b, 1)])
             register = base[c, :, block] + SCALE * added
@@ -435,7 +476,8 @@
 def body(tiles, test_field, register, velocity, shear_shift):
     field = test_field.reshape(3, CELLS, NX)
     reg = register.reshape(3, CELLS, NX)
-    zy = small(np.concatenate([rows_z(FIRST), rows_y(FIRST), rows_y(SECOND) + rows_z(SECOND)], 1))
+    ownw = small(np.concatenate([rows_y(FIRST), rows_y(SECOND) + rows_z(SECOND)], 1))
+    zy = small(np.concatenate([rows_z(FIRST), rows_y(FIRST)], 1))
     outw = small(np.concatenate([rows_out(FIRST), rows_out(SECOND)], 1))
     xw = small(np.concatenate([band(SECOND), -band(FIRST)], 0))
     edgew = small(np.concatenate([band_edges(SECOND), -band_edges(FIRST)], 0))
@@ -451,13 +493,17 @@
             pltpu.VMEM((3, 2, HALO, NX), BF),
             pltpu.VMEM((3, 4, ROWS, 128), BF),
         ),
-        in_specs=[pl.BlockSpec(memory_space=pltpu.SMEM)] * 2 + [anywhere] * 8,
+        in_specs=[pl.BlockSpec(memory_space=pltpu.SMEM)] * 2 + [anywhere] * 9,
         out_specs=(vmem,) * 4,
         scratch_shapes=[
             pltpu.VMEM((3, CELLS, NX), F32),
             pltpu.VMEM((16, 3, ROWS, NX), BF),
-            pltpu.VMEM((3, 3 * CELLS, NX), BF),
+            pltpu.VMEM((3, 2 * CELLS, NX), BF),
+            pltpu.VMEM((3 * CELLS, NX), BF),
             pltpu.VMEM((3, 2, HALO, NX), BF),
+            pltpu.VMEM((2, 2 * HALO, NX), F32),
+            pltpu.VMEM((3, ROWS, 128), F32),
+            pltpu.VMEM(ownw.shape, BF),
             pltpu.VMEM(zy.shape, BF),
             pltpu.VMEM(outw.shape, BF),
             pltpu.VMEM(xw.shape, BF),
@@ -465,11 +511,11 @@
             pltpu.VMEM(stripw.shape, BF),
             pltpu.VMEM((3, 5, ROWS, 128), BF),
             dma((5,)),
-            dma((5,)),
+            dma((6,)),
             dma((3, 15)),
             dma((3, 16)),
-            dma((2, BLOCKS)),
-            dma((2, BLOCKS)),
+            dma((2, BLOCKS + 1)),
+            dma((2, BLOCKS + 1)),
             dma((4,)),
             dma((5,)),
             dma((3,)),
@@ -480,7 +526,7 @@
             collective_id=0, has_side_effects=True, vmem_limit_bytes=54 * 2**20
         ),
         name="exchange",
-    )(shear_shift, jnp.asarray(profiles()), field, reg, velocity, zy, outw, xw, edgew, stripw)
+    )(shear_shift, jnp.asarray(profiles()), field, reg, velocity, ownw, zy, outw, xw, edgew, stripw)
 
     spread, ends = small(halo_in()), small(strip_in())
     new_field, new_register = pl.pallas_call(

time: 38 us -> 36.6 us (0.963)
  Pallas kernels: 37.2 us -> 35.8 us
    pallas_call x1, Pallas kernels: 33.5 us -> 32.1 us  [body(): pl.pallas_call(functools.partial(exchange, tiles), out_shape=(pltpu.VMEM(...]
where the time goes in v4:
time: 36.6 us; the launch traced here: 36.5 us
  Pallas kernels  35.8 us (98%)
  between operations  0.69 us (2%)
    pallas_call x1, Pallas kernels, body(): pl.pallas_call(functools.partial(exchange, tiles), out_shape=(pltpu.VMEM(...  32.1 us
    pallas_call x1, Pallas kernels, body(): pl.pallas_call(finish, out_shape=(jax.ShapeDtypeStruct((3, CELLS, NX), F3...  3.7 us

profile of v4, /device:TPU:1, one launch (start us, length us, event | category | flops | bytes accessed | tf_op | source)
XLA Modules:
  0.0 36.5 jit_solution(3383652016452479318)
XLA Ops:
  0.6 0.0 copy-start
  0.6 0.0 copy-start.1
  0.7 0.0 copy-start.2
  0.7 32.1 %exchange.1 = (f32[3,256,1024]{2,1,0:T(8,128)S(1)}, f32[3,256,1024]{2,1,0:T(8,128)S(1)}, bf16[3,2,48,1024]{3,2,1,0:T(8,128)(2,1)S(1)}, bf16[3,4,16,128]{3,2,1,0:T(8,128)(2,1)S(1)}) custom-call(s32[2]{0:T(128)} %shift.3, f32[512]{0:T(512)} %constant.24.clone.profile, f32[3,256,1024]{2,1,0:T(8,128)} %bitcast.4, f32[3,256,1024]{2,1,0:T(8,128)} %bitcast.5, ...), custom_call_target="tpu_custom_call" | custom-call | tf_op jit(solution)/shard_map/exchange/pallas_call | solution.py:488
  32.8 0.0 copy-done
  32.8 0.0 copy-done.1
  32.8 0.0 copy-done.2
  32.8 3.7 %finish.1 = (f32[3,256,1024]{2,1,0:T(8,128)}, f32[3,256,1024]{2,1,0:T(8,128)}) custom-call(s32[2]{0:T(128)S(1)} %copy-done.2, f32[3,256,1024]{2,1,0:T(8,128)S(1)} %get-tuple-element.8.base, f32[3,256,1024]{2,1,0:T(8,128)S(1)} %get-tuple-element.9.field, bf16[3,2,48,1024]{3,2,1,0:T(8,128)(2,1)S(1)} %get-tuple-element.10.halo, ...), custom_call_target="tpu_custom_call" | custom-call | tf_op jit(solution)/shard_map/finish/pallas_call | solution.py:532
Async XLA Ops:
  0.6 32.1 %copy-start = (bf16[2,128,256]{2,1,0:T(8,128)(2,1)S(1)}, bf16[2,128,256]{2,1,0:T(8,128)(2,1)}, u32[]{:S(2)}) copy-start(bf16[2,128,256]{2,1,0:T(8,128)(2,1)} %constant.26.clone.ends) | copy-start | bytes 393220
  0.6 32.1 %copy-start.1 = (bf16[256,96]{1,0:T(8,128)(2,1)S(1)}, bf16[256,96]{1,0:T(8,128)(2,1)}, u32[]{:S(2)}) copy-start(bf16[256,96]{1,0:T(8,128)(2,1)} %constant.25.clone.spread) | copy-start | bytes 147460
  0.7 32.1 %copy-start.2 = (s32[2]{0:T(128)S(1)}, s32[2]{0:T(128)}, u32[]{:S(2)}) copy-start(s32[2]{0:T(128)} %shift.3) | copy-start | bytes 28

commit v5 on v4

--- a/solution.py
+++ b/solution.py
@@ -26,9 +26,9 @@
 CELLS = NZ * ROWS
 BLOCK = 256
 BLOCKS = NX // BLOCK
-PARTS = ((0, 3), (1,), (2,))
-SPANS = ((0, 2), (2, 1), (3, 1))
-ORDER = (0, 3, 1, 2)
+PARTS = (((0, 128), (896, 128)), ((128, 512),), ((640, 256),))
+SPANS = tuple(span for part in PARTS for span in part)
+WIDTHS = tuple(sum(width for _, width in part) for part in PARTS)
 HALO = 3 * NZ
 NEAR = (-2, -1, 1, 2)
 FAR = (1, 2, 3)
@@ -134,6 +134,10 @@
     return out.reshape(-1)
 
 
+def stored_at(i):
+    return sum(width for _, width in SPANS[:i])
+
+
 def dot(a, b):
     return jnp.dot(a, b, preferred_element_type=F32)
 
@@ -142,7 +146,7 @@
     tiles, shift, profile, field_hbm, register_hbm, velocity_hbm, own_hbm, zy_hbm, out_hbm, x_hbm, edge_hbm, strip_hbm,
     base, field, halo, wide,
     register, vel, work, emf, sums, waiting, kept_strips, ownw, zy, outw, xw, edgew, stripw, near,
-    load_sem, const_sem, vsend, vrecv, hsend, hrecv, nsend, nrecv, wsend, wrecv, told,
+    load_sem, const_sem, vsend, vrecv, csend, crecv, hsend, hrecv, nsend, nrecv, wsend, wrecv, told,
 ):
     t = lax.axis_index("tile")
     k = lax.axis_index("tf")
@@ -156,12 +160,12 @@
     sibling = k + 1 - 2 * core
 
     own_velocity = []
-    for i, (low, high, to) in enumerate(((0, 1, 0), (3, 4, 1), (1, 3, 2))):
-        source = velocity_hbm.at[:, 0, :, pl.ds(low * BLOCK, (high - low) * BLOCK)]
-        target = vel.at[k, :, :, pl.ds(to * BLOCK, (high - low) * BLOCK)]
-        own_velocity.append(pltpu.make_async_copy(source, target, load_sem.at[i]))
-    load_field = pltpu.make_async_copy(field_hbm, field, load_sem.at[3])
-    load_register = pltpu.make_async_copy(register_hbm, register, load_sem.at[4])
+    for i, (start, width) in enumerate(SPANS):
+        source = velocity_hbm.at[:, 0, :, pl.ds(start, width)]
+        target = vel.at[xi, hc, :, :, pl.ds(stored_at(i), width)]
+        own_velocity.append(pltpu.make_async_copy(source, target, load_sem.at[2 + i]))
+    load_field = pltpu.make_async_copy(field_hbm, field, load_sem.at[0])
+    load_register = pltpu.make_async_copy(register_hbm, register, load_sem.at[1])
     pairs = ((own_hbm, ownw), (zy_hbm, zy), (out_hbm, outw), (x_hbm, xw), (edge_hbm, edgew), (strip_hbm, stripw))
     consts = [pltpu.make_async_copy(a, b, const_sem.at[i]) for i, (a, b) in enumerate(pairs)]
     for copy in (*own_velocity, load_field, *consts, load_register):
@@ -186,50 +190,64 @@
 
     started = []
 
-    def plane_copy(plane, part, kind, peer):
-        block = vel.at[plane, :, :, pl.ds(SPANS[part][0] * BLOCK, SPANS[part][1] * BLOCK)]
+    def lanes(part):
+        return pl.ds(sum(WIDTHS[:part]), WIDTHS[part])
+
+    def plane_copy(x, h, part, kind, peer):
+        block = vel.at[x, h, :, :, lanes(part)]
         return pltpu.make_async_remote_copy(
             src_ref=block,
             dst_ref=block,
             send_sem=vsend.at[part, kind],
-            recv_sem=vrecv.at[part, plane],
+            recv_sem=vrecv.at[part, x, h],
             device_id={"tf": peer},
         )
 
-    def send(plane, part, kind, peer):
-        copy = plane_copy(plane, part, kind, peer)
+    def send(x, h, part, kind, peer):
+        copy = plane_copy(x, h, part, kind, peer)
         copy.start()
         started.append(copy)
 
-    def arrived(plane, part):
-        plane_copy(plane, part, 0, sibling).wait_recv()
+    def arrived(x, h, part):
+        plane_copy(x, h, part, 0, sibling).wait_recv()
+
+    def row_copy(h, part, which):
+        block = vel.at[:, h, :, :, lanes(part)]
+        return pltpu.make_async_remote_copy(
+            src_ref=block,
+            dst_ref=block,
+            send_sem=csend.at[part, which],
+            recv_sem=crecv.at[part, which],
+            device_id={"tf": sibling},
+        )
+
+    def send_row(h, part, which):
+        copy = row_copy(h, part, which)
+        copy.start()
+        started.append(copy)
 
     def send_own(part):
-        for kind, peer in enumerate((partner, at_opposite, at_plus, at_minus, sibling)):
-            send(k, part, kind, peer)
+        for kind, peer in enumerate((partner, at_opposite, at_plus, at_minus)):
+            send(xi, hc, part, kind, peer)
 
     def relay(part):
-        arrived(partner, part)
-        send(partner, part, 5, at_plus)
-        send(partner, part, 6, at_minus)
-        send(partner, part, 7, sibling)
-        arrived(at_opposite, part)
-        send(at_opposite, part, 8, partner)
-        send(at_opposite, part, 9, sibling)
-        arrived(at_plus, part)
-        send(at_plus, part, 10, sibling)
-        arrived(at_minus, part)
-        send(at_minus, part, 11, sibling)
+        arrived(xi, other, part)
+        send(xi, other, part, 4, at_plus)
+        send(xi, other, part, 5, at_minus)
+        arrived(opposite, hc, part)
+        send(opposite, hc, part, 6, partner)
+        arrived(plus, hc, part)
+        arrived(minus, hc, part)
+        send_row(hc, part, 0)
 
     def last_relay(part):
-        for i, x in enumerate((plus, minus, opposite)):
-            arrived(x * 4 + other, part)
-            send(x * 4 + other, part, 12 + i, sibling)
+        for x in (plus, minus, opposite):
+            arrived(x, other, part)
+        send_row(other, part, 1)
 
     def from_sibling(part):
-        for x in range(4):
-            for h in range(2):
-                arrived(x * 4 + h * 2 + 1 - core, part)
+        for which, h in enumerate((hc, other)):
+            row_copy(h + 1 - 2 * core, part, which).wait_recv()
 
     def prepare(b):
         block = pl.ds(b * BLOCK, BLOCK)
@@ -247,13 +265,13 @@
 
         lax.fori_loop(0, NZ, plane, 0)
 
-    def emf_of(b):
-        block = pl.ds(b * BLOCK, BLOCK)
-        stored = pl.ds(ORDER.index(b) * BLOCK, BLOCK)
+    def emf_of(span):
+        block = pl.ds(*span)
+        stored = pl.ds(stored_at(SPANS.index(span)), span[1])
 
         def plane(z, carry):
             rows = pl.ds(pl.multiple_of(z * ROWS, ROWS), ROWS)
-            v = [vel[z, c, :, stored].astype(F32) for c in range(3)]
+            v = [vel[z >> 2, z & 3, c, :, stored].astype(F32) for c in range(3)]
             summed = [
                 (field[0, rows, block] + profile[k * 32 + z]).astype(BF).astype(F32),
                 (field[1, rows, block] + profile[k * 32 + 16 + z]).astype(BF).astype(F32),
@@ -266,7 +284,7 @@
                 emf[pl.ds(pl.multiple_of(i * CELLS + z * ROWS, ROWS), ROWS), block] = value.astype(BF)
             return carry
 
-        lax.fori_loop(0, NZ, plane, 0)
+        lax.fori_loop(0, NZ, plane, 0, unroll=2)
 
     def sides(array, b):
         before = array[:, b * BLOCK - 128 : b * BLOCK] if b > 0 else None
@@ -297,8 +315,8 @@
                 result -= TIME_STEP * STRETCH_RATE * field[0, :, block]
             base[c, :, block] = result
 
-    def emf_part_zy(b):
-        block = slice(b * BLOCK, (b + 1) * BLOCK)
+    def emf_part_zy(span):
+        block = pl.ds(*span)
         base[0, :, block] += SCALE * dot(zy[...], emf[: 2 * CELLS, block])
         base[1, :, block] -= SCALE * dot(zy[:, :CELLS], emf[2 * CELLS :, block])
         base[2, :, block] += SCALE * dot(zy[:, CELLS:], emf[2 * CELLS :, block])
@@ -317,19 +335,19 @@
             device_id={"tile": (t + (1, tiles - 1)[side]) % tiles},
         )
 
-    def halo_copies(b):
-        return [halo_copy(side, pl.ds(0, 2), pl.ds(b * BLOCK, BLOCK), b) for side in range(2)]
+    def halo_copies(span):
+        return [halo_copy(side, pl.ds(0, 2), pl.ds(*span), SPANS.index(span)) for side in range(2)]
 
     def y_halo_copies():
-        return [halo_copy(side, pl.ds(2, 1), pl.ds(0, NX), BLOCKS) for side in range(2)]
-
-    def halo_of(b):
-        block = slice(b * BLOCK, (b + 1) * BLOCK)
+        return [halo_copy(side, pl.ds(2, 1), pl.ds(0, NX), len(SPANS)) for side in range(2)]
+
+    def halo_of(span):
+        block = pl.ds(*span)
         for place, first in enumerate((CELLS, 2 * CELLS)):
             total = waiting[place, :, block] + dot(outw[:, :CELLS], emf[first : first + CELLS, block])
             for side in range(2):
                 sums[place, side, :, block] = total[side * HALO : (side + 1) * HALO].astype(BF)
-        for copy in halo_copies(b):
+        for copy in halo_copies(span):
             copy.start()
             started.append(copy)
 
@@ -392,7 +410,7 @@
 
     for copy in own_velocity:
         copy.wait()
-    for part in range(3):
+    for part in range(len(PARTS)):
         send_own(part)
     load_field.wait()
     for b in range(BLOCKS):
@@ -400,45 +418,45 @@
     for copy in consts:
         copy.wait()
     load_register.wait()
-    field_part(0)
-    field_part(3)
-    relay(0)
     field_strips()
-    field_part(1)
-    relay(1)
-    field_part(2)
+    for b in range(BLOCKS):
+        field_part(b)
+        if b < len(PARTS) - 1:
+            relay(b)
     for copy in y_halo_copies():
         copy.start()
         started.append(copy)
-    relay(2)
+    relay(len(PARTS) - 1)
     hear(0)
     tell(1, 2)
 
     def finish_part(part):
         last_relay(part)
         from_sibling(part)
-        for b in PARTS[part]:
-            emf_of(b)
+        for span in PARTS[part]:
+            emf_of(span)
         if part == 0:
             strips_of()
-        for b in PARTS[part]:
-            halo_of(b)
-
-    finish_part(0)
-    emf_part_zy(0)
-    finish_part(1)
-    emf_part_zy(3)
-    emf_part_x(0)
-    shifted_strips()
-    finish_part(2)
-    emf_part_zy(1)
-    emf_part_zy(2)
-    for b in (1, 2, 3):
-        emf_part_x(b)
+        for span in PARTS[part]:
+            halo_of(span)
+
+    ready, left = [], list(range(BLOCKS))
+    for part in range(len(PARTS)):
+        if part == len(PARTS) - 1:
+            shifted_strips()
+        finish_part(part)
+        for span in PARTS[part]:
+            emf_part_zy(span)
+            ready += range(span[0] // 128, (span[0] + span[1]) // 128)
+        for b in list(left):
+            tiles_read = range(max(2 * b - 1, 0), min(2 * b + 3, NX // 128))
+            if set(tiles_read) <= set(ready):
+                emf_part_x(b)
+                left.remove(b)
     for copy in y_halo_copies():
         copy.wait_recv()
-    for b in range(BLOCKS):
-        for copy in halo_copies(b):
+    for span in SPANS:
+        for copy in halo_copies(span):
             copy.wait_recv()
     for i in range(3):
         wide_copy(i).wait_recv()
@@ -497,7 +515,7 @@
         out_specs=(vmem,) * 4,
         scratch_shapes=[
             pltpu.VMEM((3, CELLS, NX), F32),
-            pltpu.VMEM((16, 3, ROWS, NX), BF),
+            pltpu.VMEM((4, 4, 3, ROWS, NX), BF),
             pltpu.VMEM((3, 2 * CELLS, NX), BF),
             pltpu.VMEM((3 * CELLS, NX), BF),
             pltpu.VMEM((3, 2, HALO, NX), BF),
@@ -510,12 +528,14 @@
             pltpu.VMEM(edgew.shape, BF),
             pltpu.VMEM(stripw.shape, BF),
             pltpu.VMEM((3, 5, ROWS, 128), BF),
-            dma((5,)),
+            dma((2 + len(SPANS),)),
             dma((6,)),
-            dma((3, 15)),
-            dma((3, 16)),
-            dma((2, BLOCKS + 1)),
-            dma((2, BLOCKS + 1)),
+            dma((len(PARTS), 7)),
+            dma((len(PARTS), 4, 4)),
+            dma((len(PARTS), 2)),
+            dma((len(PARTS), 2)),
+            dma((2, len(SPANS) + 1)),
+            dma((2, len(SPANS) + 1)),
             dma((4,)),
             dma((5,)),
             dma((3,)),

time: 36.6 us -> 34.4 us (0.940)
  Pallas kernels: 35.8 us -> 33.6 us
    pallas_call x1, Pallas kernels: 32.1 us -> 29.9 us  [body(): pl.pallas_call(functools.partial(exchange, tiles), out_shape=(pltpu.VMEM(...]
where the time goes in v5:
time: 34.4 us; the launch traced here: 34.3 us
  Pallas kernels  33.6 us (98%)
  between operations  0.69 us (2%)
    pallas_call x1, Pallas kernels, body(): pl.pallas_call(functools.partial(exchange, tiles), out_shape=(pltpu.VMEM(...  29.9 us
    pallas_call x1, Pallas kernels, body(): pl.pallas_call(finish, out_shape=(jax.ShapeDtypeStruct((3, CELLS, NX), F3...  3.7 us

profile of v5, /device:TPU:1, one launch (start us, length us, event | category | flops | bytes accessed | tf_op | source)
XLA Modules:
  0.0 34.3 jit_solution(13115813321536528553)
XLA Ops:
  0.6 0.0 copy-start
  0.6 0.0 copy-start.1
  0.7 0.0 copy-start.2
  0.7 29.9 %exchange.1 = (f32[3,256,1024]{2,1,0:T(8,128)S(1)}, f32[3,256,1024]{2,1,0:T(8,128)S(1)}, bf16[3,2,48,1024]{3,2,1,0:T(8,128)(2,1)S(1)}, bf16[3,4,16,128]{3,2,1,0:T(8,128)(2,1)S(1)}) custom-call(s32[2]{0:T(128)} %shift.3, f32[512]{0:T(512)} %constant.24.clone.profile, f32[3,256,1024]{2,1,0:T(8,128)} %bitcast.4, f32[3,256,1024]{2,1,0:T(8,128)} %bitcast.5, ...), custom_call_target="tpu_custom_call" | custom-call | tf_op jit(solution)/shard_map/exchange/pallas_call | solution.py:506
  30.6 0.0 copy-done
  30.6 0.0 copy-done.1
  30.6 0.0 copy-done.2
  30.6 3.7 %finish.1 = (f32[3,256,1024]{2,1,0:T(8,128)}, f32[3,256,1024]{2,1,0:T(8,128)}) custom-call(s32[2]{0:T(128)S(1)} %copy-done.2, f32[3,256,1024]{2,1,0:T(8,128)S(1)} %get-tuple-element.8.base, f32[3,256,1024]{2,1,0:T(8,128)S(1)} %get-tuple-element.9.field, bf16[3,2,48,1024]{3,2,1,0:T(8,128)(2,1)S(1)} %get-tuple-element.10.halo, ...), custom_call_target="tpu_custom_call" | custom-call | tf_op jit(solution)/shard_map/finish/pallas_call | solution.py:552
Async XLA Ops:
  0.6 29.9 %copy-start = (bf16[2,128,256]{2,1,0:T(8,128)(2,1)S(1)}, bf16[2,128,256]{2,1,0:T(8,128)(2,1)}, u32[]{:S(2)}) copy-start(bf16[2,128,256]{2,1,0:T(8,128)(2,1)} %constant.26.clone.ends) | copy-start | bytes 393220
  0.6 29.9 %copy-start.1 = (bf16[256,96]{1,0:T(8,128)(2,1)S(1)}, bf16[256,96]{1,0:T(8,128)(2,1)}, u32[]{:S(2)}) copy-start(bf16[256,96]{1,0:T(8,128)(2,1)} %constant.25.clone.spread) | copy-start | bytes 147460
  0.7 29.9 %copy-start.2 = (s32[2]{0:T(128)S(1)}, s32[2]{0:T(128)}, u32[]{:S(2)}) copy-start(s32[2]{0:T(128)} %shift.3) | copy-start | bytes 28
